TPU v7x, 32 devices: a whole 2x2x4 slice. The times are simulated.
32 devices in a mesh: groups: 2 (over y), sky: 4 (over z), shell: 2 (over x), sub: 2 (over core).
Axes of the slice: x: 2, y: 2, z: 4, core: 2. Of those that a mesh axis runs over, the one named last changes fastest.
Arguments:
- part_cycle: int32 [2, 2048, 256], P('shell', ('sky', 'sub')), may hold values from 0 to 1
- part_pixel: int32 [2, 2048, 256], P('shell', ('sky', 'sub')), may hold values from 0 to 127
- part_mass: float32 [2, 2048, 256], P('shell', ('sky', 'sub')), may hold values from 0.3 to 3
- tile_block: int32 [2, 2048, 1], P('shell', ('sky', 'sub')), may hold values from 0 to 7; in each aligned block of 256 rows (0 to 255, 256 to 511, ..., all dimensions but the last counted through in order) at most 128 rows name the same one
- tile_shell: int32 [2, 2048], P('shell', ('sky', 'sub')), may hold values from 0 to 1
- tile_pixel: int32 [2, 2048], P('shell', ('sky', 'sub')), may hold values from 0 to 63
- harmonic_basis: bfloat16 [128, 16, 4096], P('sky', 'sub'), may hold values from -1.5 to 1.5
- lens_weight: float32 [4, 4], replicated, may hold values from 0.2 to 1
Outputs:
- convergence: float32 [8, 128, 2, 4096], P(('groups', 'shell'), 'sky', None, 'sub'), parts along dimension 0
There are 2 independent parts, one for each index of `groups`. A program takes and returns all parts, laid end to end along the dimension named above; an argument that names none is the same for every part. Nothing has to cross between parts.
Inputs may be any that keep to these rules, and one draw needn't show every extreme that they name: `tile_block`: among the rows of one device no cycle block is named by more than 128 tiles, and in some device one block is named by exactly 128.
All inputs are finite; a program needn't handle non-finite values.
Results may differ from a plain program's by a relative error of at most 0.0015.
Values may be sent and summed in bfloat16 or wider, within the bound.
A program may use at most 192 MiB of HBM per device.

v0:
```python
import math

import jax
import jax.numpy as jnp
from jax import lax
from jax.sharding import PartitionSpec as P

NP = 8192
M = 128
TP = 128
CYCLE_DEV = 2
SHELL_DEV = 2


precise = lax.Precision.HIGHEST


def deposit(cycle_index, pixel_index, masses):
    cycle_axis = jnp.arange(CYCLE_DEV, dtype=jnp.float32)
    pixel_axis = jnp.arange(TP, dtype=jnp.float32)
    cycle_part = jnp.exp(
        -0.5 * (cycle_axis[None, None, :] - cycle_index.astype(jnp.float32)[:, :, None]) ** 2
    )
    pixel_part = jnp.exp(
        -((pixel_axis[None, None, :] - pixel_index.astype(jnp.float32)[:, :, None]) ** 2) / 18.0
    )
    weighted = pixel_part * masses[:, :, None]
    return jnp.einsum("tpk,tpj->tkj", cycle_part, weighted, precision=precise)


def fourier_table(count):
    pixels = jnp.arange(count, dtype=jnp.int32)
    orders = jnp.arange(M, dtype=jnp.int32)
    phases = pixels[:, None] * orders[None, :] % NP
    angles = phases.astype(jnp.float32) * (2.0 * math.pi / NP)
    return jnp.concatenate([jnp.cos(angles), -jnp.sin(angles)], axis=1)


def body(
    part_cycle,
    part_pixel,
    part_mass,
    tile_block,
    tile_shell,
    tile_pixel,
    harmonic_basis,
    lens_weight,
):
    sky_count = lax.axis_size("sky")
    sub_count = lax.axis_size("sub")
    owners = sky_count * sub_count
    tile_count = part_cycle.shape[1]
    tile_sums = deposit(part_cycle[0], part_pixel[0], part_mass[0]).reshape(
        tile_count, CYCLE_DEV * TP
    )
    local_modes = jnp.dot(
        tile_sums.reshape(tile_count * CYCLE_DEV, TP), fourier_table(TP), precision=precise
    )
    local_modes = local_modes.reshape(tile_count, CYCLE_DEV, 2, M)
    orders = jnp.arange(M, dtype=jnp.int32)
    turns = tile_pixel[0][:, None] * TP * orders[None, :] % NP
    angles = turns.astype(jnp.float32) * (2.0 * math.pi / NP)
    cosine = jnp.cos(angles)[:, None, :]
    sine = -jnp.sin(angles)[:, None, :]
    real_part = local_modes[:, :, 0, :]
    imag_part = local_modes[:, :, 1, :]
    rotated = jnp.stack(
        [real_part * cosine - imag_part * sine, real_part * sine + imag_part * cosine], axis=2
    )
    bin_key = tile_shell[0] * owners + tile_block[0, :, 0]
    bin_hot = (bin_key[None, :] == jnp.arange(SHELL_DEV * owners, dtype=jnp.int32)[:, None]).astype(
        jnp.float32
    )
    binned = jnp.dot(bin_hot, rotated.reshape(tile_count, CYCLE_DEV * 2 * M), precision=precise)
    binned = binned.reshape(SHELL_DEV, owners, CYCLE_DEV, 2, M).transpose(4, 0, 3, 1, 2)
    binned = binned.reshape(M, SHELL_DEV, 2, owners * CYCLE_DEV)
    order_part = lax.psum_scatter(binned, "sky", scatter_dimension=0, tiled=True)
    cycle_part = lax.psum_scatter(order_part, "sub", scatter_dimension=3, tiled=True)
    by_order = (cycle_part * (2.0 * math.pi / NP)).astype(jnp.bfloat16)
    harmonics = jnp.einsum(
        "mrl,mscr->mscl", harmonic_basis, by_order, preferred_element_type=jnp.float32
    )
    halves = lax.psum_scatter(harmonics, "sub", scatter_dimension=3, tiled=True)
    shell_index = lax.axis_index("shell")
    sources = lens_weight.shape[0]
    first_shell = shell_index * SHELL_DEV
    local_weight = lax.dynamic_slice_in_dim(lens_weight, first_shell, SHELL_DEV, 1)
    source_ids = jnp.arange(sources, dtype=jnp.int32)
    shell_ids = first_shell + jnp.arange(SHELL_DEV, dtype=jnp.int32)
    local_weight = local_weight * (shell_ids[None, :] <= source_ids[:, None]).astype(jnp.float32)
    planes = jnp.einsum("js,mscl->jmcl", local_weight, halves, precision=precise)
    per_device = sources // lax.axis_size("shell")
    totals = lax.psum(planes, "shell")
    result = lax.dynamic_slice_in_dim(totals, shell_index * per_device, per_device, 0)
    return result


def solution(mesh):
    return jax.shard_map(
        body,
        mesh=mesh,
        in_specs=(
            P("shell", ("sky", "sub"), None),
            P("shell", ("sky", "sub"), None),
            P("shell", ("sky", "sub"), None),
            P("shell", ("sky", "sub"), None),
            P("shell", ("sky", "sub")),
            P("shell", ("sky", "sub")),
            P("sky", "sub", None),
            P(),
        ),
        out_specs=P(("groups", "shell"), "sky", None, "sub"),
        check_vma=False,
    )
```

profile of v0, /device:TPU:0, one launch (start us, length us, event | category | flops | bytes accessed | tf_op | source)
XLA Modules:
  0.0 695.1 jit_solution(14472158354454681368)
XLA Ops:
  6.5 0.0 copy-start
  6.5 0.0 reduce-scatter.10.cloned.1.call-start
  6.5 0.3 sine_negate_fusion.1
  6.8 0.8 broadcast_multiply_fusion
  7.7 0.5 fusion.38
  8.2 0.0 copy-start.2
  8.2 0.0 copy-start.3
  8.2 1.1 convert_bitcast_fusion
  9.3 35.0 %fusion.15 = f32[256,2,128,1]{2,1,0,3:T(2,128)S(1)} fusion(f32[256,256]{1,0:T(8,128)} %bitcast.57, f32[256,256]{1,0:T(8,128)S(1)} %get-tuple-element.11, f32[256,256]{1,0:T(8,128)S(1)} %get-tuple-element.12), kind=kOutput, calls=%fused_computation.15 | convolution fusion | flops 243662848 | bytes 1048576 | tf_op jit(solution)/shard_map/tpk,tpj->tkj/dot_general | solution.py:28
  44.4 0.6 fusion.25
  45.0 0.0 copy-done.2
  45.0 0.0 copy-done.3
  45.0 0.1 multiply_subtract_fusion
  45.1 0.3 convolution_bitcast_fusion
  45.4 0.7 copy.30
  46.2 0.0 reduce-scatter.10.cloned.1.call-update
  46.2 0.0 reduce-scatter.8.cloned.1.call-start
  46.3 21.8 %reduce-scatter.10.cloned.1.call-done = f32[32,64]{1,0:T(8,128)} async-done(((f32[128,64]{1,0:T(8,128)}), f32[32,64]{1,0:T(8,128)}) %reduce-scatter.10.cloned.1.call-update) | async-done | bytes 8208
  68.1 1.4 copy.31
  69.5 0.0 reduce-scatter.8.cloned.1.call-update
  69.5 0.0 reduce-scatter.12.cloned.1.call-start
  69.6 6.4 reduce-scatter.8.cloned.1.call-done
  75.9 0.7 multiply_convert_fusion
  76.6 0.1 copy.16
  76.8 0.0 copy-done
  76.8 2.1 fusion.13
  78.8 139.1 %copy.28 = f32[32,2,2,4096]{1,2,0,3:T(2,128)} copy(f32[32,2,2,4096]{3,1,2,0:T(2,128)} %fusion.13) | data formatting | bytes 4194304
  218.0 165.9 %reshape.116 = f32[4096,128]{1,0:T(8,128)} reshape(f32[4096,32,2,2]{3,2,1,0:T(2,128)} %bitcast.23) | data formatting | bytes 4194304
  383.8 0.0 reduce-scatter.12.cloned.1.call-update
  383.8 0.0 all-reduce.2.cloned.1.call-start
  383.9 0.0 copy-start.1
  383.9 10.8 %reduce-scatter.12.cloned.1.call-done = f32[2048,128]{1,0:T(8,128)} async-done(((f32[4096,128]{1,0:T(8,128)}), f32[2048,128]{1,0:T(8,128)}) %reduce-scatter.12.cloned.1.call-update) | async-done | bytes 1048592
  394.8 105.0 %reshape.117 = f32[2048,32,2,2]{3,2,1,0:T(2,128)} reshape(f32[2048,128]{1,0:T(8,128)} %reduce-scatter.12.cloned.1.call-done) | data formatting | bytes 2097152
  499.7 0.0 copy-done.1
  499.7 120.6 %fusion = f32[4,32,2,2048]{3,0,2,1:T(4,128)} fusion(f32[32,2,2,2048]{1,2,0,3:T(2,128)} %bitcast.24, f32[4,4]{1,0:T(4,128)S(1)} %copy-done.1, s32[]{:T(128)S(6)} %select_n.26, s32[2]{0:T(128)S(1)} %iota_add_fusion), kind=kOutput, calls=%fused_computation | convolution fusion | flops 12582928 | bytes 3145804 | tf_op jit(solution)/shard_map/js,mscl->jmcl/dot_general | solution.py:91
  620.3 0.0 all-reduce.2.cloned.1.call-update
  620.3 64.2 %all-reduce.2.cloned.1.call-done = f32[4,32,2,2048]{3,0,2,1:T(4,128)} async-done(((f32[4,32,2,2048]{3,0,2,1:T(4,128)}), f32[4,32,2,2048]{3,0,2,1:T(4,128)}) %all-reduce.2.cloned.1.call-update) | async-done | bytes 2097168 | tf_op jit(solution)/shard_map/psum | solution.py:93
  684.6 2.2 constant_dynamic-slice_fusion
  686.7 1.8 copy.18
  (5 shorter events, 0.1 us)
Async XLA Ops:
  6.5 70.2 %copy-start = (bf16[32,8,4096]{2,1,0:T(8,128)(2,1)S(1)}, bf16[32,8,4096]{2,1,0:T(8,128)(2,1)}, u32[]{:S(2)}) copy-start(bf16[32,8,4096]{2,1,0:T(8,128)(2,1)} %param.14) | copy-start | bytes 6291460
  6.5 61.5 %reduce-scatter.10.cloned.1.call-start = ((), (), s32[]{:S(2)}) async-start(), calls=%async_computation.5 | async-start | bytes 81920
  8.2 36.8 %copy-start.2 = (s32[1,256,1]{1,2,0:T(1,128)S(1)}, s32[1,256,1]{1,2,0:T(1,128)}, u32[]{:S(2)}) copy-start(s32[1,256,1]{1,2,0:T(1,128)} %param.11) | copy-start | bytes 3076
  8.2 36.8 %copy-start.3 = (s32[1,256]{1,0:T(1,128)S(1)}, s32[1,256]{1,0:T(1,128)}, u32[]{:S(2)}) copy-start(s32[1,256]{1,0:T(1,128)} %param.12) | copy-start | bytes 3076
  46.2 29.7 %reduce-scatter.8.cloned.1.call-start = ((), (), s32[]{:S(2)}) async-start(), calls=%async_computation.3 | async-start | bytes 49152 | tf_op jit(solution)/shard_map/reduce_scatter | solution.py:78
  69.5 325.3 %reduce-scatter.12.cloned.1.call-start = ((), (), s32[]{:S(2)}) async-start(), calls=%async_computation.6 | async-start | bytes 3145728
  383.8 300.7 %all-reduce.2.cloned.1.call-start = ((), (), s32[]{:S(2)}) async-start(), calls=%async_computation.4 | async-start | bytes 4194304 | tf_op jit(solution)/shard_map/psum | solution.py:93
  383.9 115.8 %copy-start.1 = (f32[4,4]{1,0:T(4,128)S(1)}, f32[4,4]{1,0:T(4,128)}, u32[]{:S(2)}) copy-start(f32[4,4]{1,0:T(4,128)} %param.15) | copy-start | bytes 196
Sparse Core Ops, SparseCore 0:
  46.3 21.6 reduce-scatter.9
  70.3 5.5 reduce-scatter.7
  384.0 10.7 reduce-scatter.11
  620.5 64.0 all-reduce.1
where the time goes:
time: 706 us; the launch traced here: 695 us
  local copies, waits for them, and re-layouts  416 us (59%)
  matrix products  159 us (23%)
  waiting for transfers between devices  103 us (15%)
  between operations  13.3 us (2%)
    unnamed x13, local copies, waits for them, and re-layouts  412 us
    dot_general x1, matrix products, body(): jnp.einsum('js,mscl->jmcl', local_weight, halves, precision=precise)  121 us
    psum x1, waiting for transfers between devices, body(): totals = lax.psum(planes, 'shell')  64.2 us
    dot_general x1, matrix products, deposit(): return jnp.einsum('tpk,tpj->tkj', cycle_part, weighted, precision=precise)  35 us
    unnamed x6, waiting for transfers between devices  32.7 us
  transfers between devices with their start and end apart: 4, of which 4 were waited for; matrix products, arithmetic and copies ran while one was open for 0% of the time, Pallas kernels for 0%

commit v1 on v0

v1 whole, which is shorter than its diff:
```python
import functools
import math

import jax
import jax.numpy as jnp
import numpy as np
from jax import lax
from jax.experimental import pallas as pl
from jax.experimental.pallas import tpu as pltpu
from jax.sharding import PartitionSpec as P

NP = 8192
M = 128
TP = 128
CYCLE_DEV = 2
SHELL_DEV = 2
NBLK = NP // TP

precise = lax.Precision.HIGHEST
MESH = pl.DeviceIdType.MESH


def tables():
    pixel = np.arange(TP, dtype=np.float64)
    smooth = np.exp(-((pixel[:, None] - pixel[None, :]) ** 2) / 18.0)
    orders = np.arange(M)
    angle = 2.0 * math.pi * ((np.arange(TP)[:, None] * orders[None, :]) % NP) / NP
    real, imag = smooth @ np.cos(angle), -(smooth @ np.sin(angle))
    straight = np.stack([real, imag], axis=2).reshape(TP, 2 * M).T
    crossed = np.stack([-imag, real], axis=2).reshape(TP, 2 * M).T
    turn = 2.0 * math.pi * ((np.arange(NBLK)[:, None] * TP * orders[None, :]) % NP) / NP
    cosine = np.repeat(np.cos(turn), 2, axis=1).T
    sine = np.repeat(-np.sin(turn), 2, axis=1).T
    spectrum = np.concatenate([straight, crossed], axis=0).astype(np.float32)
    turns = np.concatenate([cosine, sine], axis=0).astype(np.float32)
    return spectrum, turns


def deposit_kernel(
    sky_count, owners, cycle_ref, pixel_ref, mass_ref, block_ref, shell_ref, place_ref, spectrum_ref,
    turns_ref, out_ref, pixel_t, mass0_t, mass1_t, hist_ref,
):
    tiles, particles = pixel_ref.shape
    lanes = 128
    rows = 64
    masses = mass_ref[...]
    first = cycle_ref[...] == 0
    for held, value in (
        (pixel_t, pixel_ref[...]),
        (mass0_t, jnp.where(first, masses, 0.0)),
        (mass1_t, jnp.where(first, 0.0, masses)),
    ):
        turned = value.T
        for side in range(tiles // lanes):
            held[side] = turned[:, side * lanes : (side + 1) * lanes]
    for side in range(tiles // lanes):
        columns = slice(side * lanes, (side + 1) * lanes)
        for top in range(0, TP, rows):
            ids = lax.broadcasted_iota(jnp.int32, (rows, lanes), 0) + top

            def step(p, sums):
                here = jnp.broadcast_to(pixel_t[side, pl.ds(p, 1), :], (rows, lanes)) == ids
                one = jnp.broadcast_to(mass0_t[side, pl.ds(p, 1), :], (rows, lanes))
                two = jnp.broadcast_to(mass1_t[side, pl.ds(p, 1), :], (rows, lanes))
                return sums[0] + jnp.where(here, one, 0.0), sums[1] + jnp.where(here, two, 0.0)

            zero = jnp.zeros((rows, lanes), jnp.float32)
            one, two = lax.fori_loop(0, particles, step, (zero, zero), unroll=8)
            hist_ref[0, top : top + rows, columns] = one
            hist_ref[1, top : top + rows, columns] = two
    position = (
        lax.broadcasted_iota(jnp.int32, (NBLK, tiles), 0) == place_ref[...]
    ).astype(jnp.float32)
    turns = jnp.dot(turns_ref[...], position, precision=precise, preferred_element_type=jnp.float32)
    cosine, sine = turns[: 2 * M], turns[2 * M :]
    near = math.exp(-0.5)
    turned = []
    for k in range(CYCLE_DEV):
        mixed = hist_ref[k] + near * hist_ref[1 - k]
        modes = jnp.dot(
            spectrum_ref[...], mixed, precision=precise, preferred_element_type=jnp.float32
        )
        turned.append(modes[: 2 * M] * cosine + modes[2 * M :] * sine)
    share = 2 * M // sky_count
    stacked = jnp.concatenate(
        [turned[k][z * share : (z + 1) * share] for z in range(sky_count) for k in range(CYCLE_DEV)],
        axis=0,
    )
    bins = SHELL_DEV * owners
    key = shell_ref[...] * owners + block_ref[...]
    hot = (lax.broadcasted_iota(jnp.int32, (bins, tiles), 0) == key).astype(jnp.float32)
    binned = lax.dot_general(
        hot, stacked, (((1,), (1,)), ((), ())), precision=precise, preferred_element_type=jnp.float32
    )
    width = CYCLE_DEV * share
    for z in range(sky_count):
        out_ref[z] = binned[:, z * width : (z + 1) * width]


def mode_kernel(
    counts, per, blocks, cycles, weight_ref, parts_ref, basis_ref, out_ref,
    halves, arrived, own_sem, half_send, half_recv, part_send, part_recv,
):
    shell_count, sky_count, sub_count = counts
    shell, sky, sub = lax.axis_index("shell"), lax.axis_index("sky"), lax.axis_index("sub")
    peers = shell_count * sky_count * sub_count
    me = (shell * sky_count + sky) * sub_count + sub
    degrees = halves.shape[2]
    orders = basis_ref.shape[0] // cycles

    def place(rank):
        return dict(
            shell=rank // (sky_count * sub_count),
            sky=rank // sub_count % sky_count,
            sub=rank % sub_count,
        )

    barrier = pltpu.get_barrier_semaphore()

    @pl.loop(1, peers)
    def _(j):
        pl.semaphore_signal(
            barrier, inc=1, device_id=place((me + j) % peers), device_id_type=MESH
        )

    pl.semaphore_wait(barrier, peers - 1)

    def send(j):
        target = place((me + j) % peers)
        return pltpu.make_async_remote_copy(
            src_ref=parts_ref.at[target["sky"]],
            dst_ref=arrived.at[me],
            send_sem=part_send.at[j],
            recv_sem=part_recv.at[j],
            device_id=target,
            device_id_type=MESH,
        )

    def expect(j):
        source = (me + peers - j) % peers
        return pltpu.make_async_remote_copy(
            src_ref=parts_ref.at[0],
            dst_ref=arrived.at[source],
            send_sem=part_send.at[j],
            recv_sem=part_recv.at[j],
            device_id=place(source),
            device_id_type=MESH,
        )

    @pl.loop(1, peers)
    def _(j):
        send(j).start()

    def half(j):
        target = (sub + j) % sub_count
        return pltpu.make_async_remote_copy(
            src_ref=basis_ref.at[:, pl.ds(pl.multiple_of(target * degrees, degrees), degrees)],
            dst_ref=halves.at[sub],
            send_sem=half_send.at[j],
            recv_sem=half_recv.at[j],
            device_id={"sub": target},
            device_id_type=MESH,
        )

    def expect_half(j):
        source = (sub + sub_count - j) % sub_count
        return pltpu.make_async_remote_copy(
            src_ref=basis_ref.at[:, pl.ds(0, degrees)],
            dst_ref=halves.at[source],
            send_sem=half_send.at[j],
            recv_sem=half_recv.at[j],
            device_id={"sub": source},
            device_id_type=MESH,
        )

    for j in range(1, sub_count):
        half(j).start()
    own = pltpu.make_async_copy(
        basis_ref.at[:, pl.ds(pl.multiple_of(sub * degrees, degrees), degrees)],
        halves.at[sub],
        own_sem,
    )
    own.start()
    arrived[me] = parts_ref[sky]

    @pl.loop(1, peers)
    def _(j):
        expect(j).wait_recv()

    group = sky_count * sub_count
    folded = [None] * per
    for x in range(shell_count):
        total = jnp.sum(arrived[x * group : (x + 1) * group], axis=0)
        modes = (total * (2.0 * math.pi / NP)).astype(jnp.bfloat16).astype(jnp.float32)
        for s in range(SHELL_DEV):
            part = modes[s * blocks : (s + 1) * blocks]
            lens = x * SHELL_DEV + s
            for i in range(per):
                source = shell * per + i
                weight = jnp.where(lens <= source, weight_ref[source, lens], 0.0)
                term = weight * part
                folded[i] = term if folded[i] is None else folded[i] + term
    coefficients = jnp.concatenate(folded, axis=0).T
    high = coefficients.astype(jnp.bfloat16)
    low = (coefficients - high.astype(jnp.float32)).astype(jnp.bfloat16)
    depth = orders * cycles
    span = 2 * orders
    lane = lax.broadcasted_iota(jnp.int32, (per * blocks, depth), 1)
    row = lax.broadcasted_iota(jnp.int32, (per * blocks, depth), 0)
    lane_out = lax.broadcasted_iota(jnp.int32, (span, depth), 1)
    diagonal = lane_out // cycles == lax.broadcasted_iota(jnp.int32, (span, depth), 0) // 2
    even = lane_out % CYCLE_DEV == 0
    left = []
    for h in range(sub_count):
        rows = []
        for piece in (high, low):
            for i in range(per):
                block = i * blocks + h * (cycles // CYCLE_DEV) + lane % cycles // CYCLE_DEV
                pick = (row == block).astype(jnp.float32).astype(jnp.bfloat16)
                spread = jnp.dot(piece, pick, preferred_element_type=jnp.float32)
                chosen = jnp.where(even, spread[:span], spread[span:])
                rows.append(jnp.where(diagonal, chosen, 0.0).astype(jnp.bfloat16))
        left.append(jnp.concatenate(rows, axis=0))
    own.wait()
    for j in range(1, sub_count):
        expect_half(j).wait_recv()
    step = 512
    for first in range(0, degrees, step):
        columns = slice(first, first + step)
        result = None
        for h in range(sub_count):
            term = jnp.dot(left[h], halves[h, :, columns], preferred_element_type=jnp.float32)
            result = term if result is None else result + term
        result = result[: per * span] + result[per * span :]
        for i in range(per):
            out_ref[i, :, columns] = result[i * span : (i + 1) * span]
    for j in range(1, sub_count):
        half(j).wait_send()

    @pl.loop(1, peers)
    def _(j):
        send(j).wait_send()


def body(
    part_cycle,
    part_pixel,
    part_mass,
    tile_block,
    tile_shell,
    tile_pixel,
    harmonic_basis,
    lens_weight,
):
    shell_count, sky_count, sub_count = (
        lax.axis_size("shell"),
        lax.axis_size("sky"),
        lax.axis_size("sub"),
    )
    owners = sky_count * sub_count
    peers = shell_count * owners
    tiles, particles = part_cycle.shape[1:]
    orders, cycles, degrees = harmonic_basis.shape
    per = lens_weight.shape[0] // shell_count
    share = degrees // sub_count
    bins = SHELL_DEV * owners
    width = 2 * CYCLE_DEV * orders
    spectrum, turns = tables()
    vmem = pl.BlockSpec(memory_space=pltpu.VMEM)
    parts = pl.pallas_call(
        functools.partial(deposit_kernel, sky_count, owners),
        out_shape=jax.ShapeDtypeStruct((sky_count, bins, width), jnp.float32),
        in_specs=[vmem] * 8,
        out_specs=vmem,
        scratch_shapes=[
            pltpu.VMEM((tiles // 128, particles, 128), jnp.int32),
            pltpu.VMEM((tiles // 128, particles, 128), jnp.float32),
            pltpu.VMEM((tiles // 128, particles, 128), jnp.float32),
            pltpu.VMEM((CYCLE_DEV, TP, tiles), jnp.float32),
        ],
        compiler_params=pltpu.CompilerParams(vmem_limit_bytes=24 << 20),
        name="deposit",
    )(
        part_cycle[0],
        part_pixel[0],
        part_mass[0],
        tile_block.reshape(1, tiles),
        tile_shell,
        tile_pixel,
        spectrum,
        turns,
    )
    result = pl.pallas_call(
        functools.partial(mode_kernel, (shell_count, sky_count, sub_count), per, owners, cycles),
        out_shape=jax.ShapeDtypeStruct((per, 2 * orders, share), jnp.float32),
        in_specs=[pl.BlockSpec(memory_space=pltpu.SMEM), vmem, pl.BlockSpec(memory_space=pl.ANY)],
        out_specs=vmem,
        scratch_shapes=[
            pltpu.VMEM((sub_count, orders * cycles, share), jnp.bfloat16),
            pltpu.VMEM((peers, bins, width), jnp.float32),
            pltpu.SemaphoreType.DMA,
            pltpu.SemaphoreType.DMA((sub_count,)),
            pltpu.SemaphoreType.DMA((sub_count,)),
            pltpu.SemaphoreType.DMA((peers,)),
            pltpu.SemaphoreType.DMA((peers,)),
        ],
        compiler_params=pltpu.CompilerParams(
            collective_id=0, has_side_effects=True, vmem_limit_bytes=24 << 20
        ),
        name="modes",
    )(lens_weight, parts, harmonic_basis.reshape(orders * cycles, degrees))
    return result.reshape(per, orders, 2, share)


def solution(mesh):
    return jax.shard_map(
        body,
        mesh=mesh,
        in_specs=(
            P("shell", ("sky", "sub"), None),
            P("shell", ("sky", "sub"), None),
            P("shell", ("sky", "sub"), None),
            P("shell", ("sky", "sub"), None),
            P("shell", ("sky", "sub")),
            P("shell", ("sky", "sub")),
            P("sky", "sub", None),
            P(),
        ),
        out_specs=P(("groups", "shell"), "sky", None, "sub"),
        check_vma=False,
    )
```

time: 706 us -> 32.1 us (0.05); the launches traced: 695 us -> 31.7 us
  local copies, waits for them, and re-layouts: 416 us -> 10.7 us
  matrix products: 159 us -> 0 us
  waiting for transfers between devices: 103 us -> 0 us
  Pallas kernels: 0 us -> 21 us
  between operations: 13.3 us -> 0.02 us
    unnamed x13 -> x20, local copies, waits for them, and re-layouts: 412 us -> 9.09 us
    dot_general x5 -> x0, matrix products: 159 us -> none  [the longest x1 121 us: body(): jnp.einsum('js,mscl->jmcl', local_weight, halves, precision=precise)]
    psum x1 -> x0, waiting for transfers between devices: 64.2 us -> none  [body(): totals = lax.psum(planes, 'shell')]
    unnamed x6 -> x0, waiting for transfers between devices: 32.7 us -> none
    pallas_call x0 -> x2, Pallas kernels: none -> 21 us  [the longest x1 12.3 us: body(): pl.pallas_call(functools.partial(mode_kernel, (shell_count, sky_count, su...]
  transfers between devices with their start and end apart: 4 -> 0, of which waited for: 4 -> 0; matrix products, arithmetic and copies ran while one was open for 0% -> 0% of each run, Pallas kernels for 0% -> 0%
where the time goes in v1:
time: 32.1 us; the launch traced here: 31.7 us
  Pallas kernels  21 us (65%)
  local copies, waits for them, and re-layouts  10.7 us (33%)
    pallas_call x1, Pallas kernels, body(): pl.pallas_call(functools.partial(mode_kernel, (shell_count, sky_count, su...  12.3 us
    unnamed x20, local copies, waits for them, and re-layouts  9.09 us
    pallas_call x1, Pallas kernels, body(): pl.pallas_call(functools.partial(deposit_kernel, sky_count, owners), out_...  8.73 us
    reshape x1, local copies, waits for them, and re-layouts, body(): return result.reshape(per, orders, 2, share)  1.59 us

profile of v1, /device:TPU:0, one launch (start us, length us, event | category | flops | bytes accessed | tf_op | source)
XLA Modules:
  0.0 31.7 jit_solution(1048587774122900908)
XLA Ops:
  0.0 0.0 copy-start.1
  0.0 0.9 %copy-done.1 = s32[1,256,256]{2,1,0:T(8,128)S(1)} copy-done((s32[1,256,256]{2,1,0:T(8,128)S(1)}, s32[1,256,256]{2,1,0:T(8,128)}, u32[]{:S(2)}) %copy-start.1) | copy-done | bytes 262168
  1.0 0.0 copy-start.2
  1.0 0.9 %copy-done.2 = s32[1,256,256]{2,1,0:T(8,128)S(1)} copy-done((s32[1,256,256]{2,1,0:T(8,128)S(1)}, s32[1,256,256]{2,1,0:T(8,128)}, u32[]{:S(2)}) %copy-start.2) | copy-done | bytes 262168
  1.9 0.0 copy-start.3
  1.9 0.9 %copy-done.3 = f32[1,256,256]{2,1,0:T(8,128)S(1)} copy-done((f32[1,256,256]{2,1,0:T(8,128)S(1)}, f32[1,256,256]{2,1,0:T(8,128)}, u32[]{:S(2)}) %copy-start.3) | copy-done | bytes 262168
  2.9 0.0 copy-start.4
  2.9 0.9 %copy-done.4 = f32[512,64]{1,0:T(8,128)S(1)} copy-done((f32[512,64]{1,0:T(8,128)S(1)}, f32[512,64]{1,0:T(8,128)}, u32[]{:S(2)}) %copy-start.4) | copy-done | bytes 131096
  3.8 0.0 copy-start.5
  3.8 0.9 %copy-done.5 = f32[512,128]{1,0:T(8,128)S(1)} copy-done((f32[512,128]{1,0:T(8,128)S(1)}, f32[512,128]{1,0:T(8,128)}, u32[]{:S(2)}) %copy-start.5) | copy-done | bytes 262168
  4.8 0.0 copy-start.7
  4.8 0.7 %copy-done.7 = s32[1,256,1]{1,2,0:T(1,128)S(1)} copy-done((s32[1,256,1]{1,2,0:T(1,128)S(1)}, s32[1,256,1]{1,2,0:T(1,128)}, u32[]{:S(2)}) %copy-start.7) | copy-done | bytes 1048
  5.4 0.0 copy-start.8
  5.4 0.7 %copy-done.8 = s32[1,256]{1,0:T(1,128)S(1)} copy-done((s32[1,256]{1,0:T(1,128)S(1)}, s32[1,256]{1,0:T(1,128)}, u32[]{:S(2)}) %copy-start.8) | copy-done | bytes 1048
  6.1 0.0 copy-start.9
  6.1 0.7 %copy-done.9 = s32[1,256]{1,0:T(1,128)S(1)} copy-done((s32[1,256]{1,0:T(1,128)S(1)}, s32[1,256]{1,0:T(1,128)}, u32[]{:S(2)}) %copy-start.9) | copy-done | bytes 1048
  6.8 8.7 %deposit.1.parts_ref = f32[4,16,128]{2,1,0:T(8,128)S(1)} custom-call(s32[256,256]{1,0:T(8,128)S(1)} %bitcast.6, s32[256,256]{1,0:T(8,128)S(1)} %bitcast.7, f32[256,256]{1,0:T(8,128)S(1)} %bitcast.8, s32[1,256]{1,0:T(1,128)S(1)} %bitcast.9, s32[1,256]{1,0:T(1,128)S(1)} %copy-done.8, s32[1,256]{1,0:T(1,128)S(1)} %copy-done.9, f32[512,128]{1,0:T(8,128)S(1)} %copy-done.5, ...), custom_call_target="tpu_custom_call" | custom-call | tf_op jit(solution)/shard_map/deposit/pallas_call | solution.py:270
  15.5 0.0 copy-start
  15.5 1.6 %copy-done = bf16[32,8,4096]{2,1,0:T(8,128)(2,1)S(1)} copy-done((bf16[32,8,4096]{2,1,0:T(8,128)(2,1)S(1)}, bf16[32,8,4096]{2,1,0:T(8,128)(2,1)}, u32[]{:S(2)}) %copy-start) | copy-done | bytes 2097176
  17.2 0.0 copy-start.6
  17.2 0.7 %copy-done.6 = f32[4,4]{1,0:T(4,128)S(1)} copy-done((f32[4,4]{1,0:T(4,128)S(1)}, f32[4,4]{1,0:T(4,128)}, u32[]{:S(2)}) %copy-start.6) | copy-done | bytes 88
  17.8 12.3 %modes.1 = f32[2,64,2048]{2,1,0:T(8,128)S(1)} custom-call(f32[4,4]{1,0:T(4,128)S(1)} %copy-done.6, f32[4,16,128]{2,1,0:T(8,128)S(1)} %deposit.1.parts_ref, bf16[256,4096]{1,0:T(8,128)(2,1)S(1)} %bitcast.5), custom_call_target="tpu_custom_call" | custom-call | tf_op jit(solution)/shard_map/modes/pallas_call | solution.py:293
  30.1 1.6 %reshape.11 = f32[2,32,2,2048]{3,2,1,0:T(2,128)} reshape(f32[2,64,2048]{2,1,0:T(8,128)S(1)} %modes.1) | data formatting | bytes 2097152 | tf_op jit(solution)/shard_map/reshape | solution.py:312
Async XLA Ops:
  0.0 0.9 %copy-start.1 = (s32[1,256,256]{2,1,0:T(8,128)S(1)}, s32[1,256,256]{2,1,0:T(8,128)}, u32[]{:S(2)}) copy-start(s32[1,256,256]{2,1,0:T(8,128)} %param.10) | copy-start | bytes 786436
  1.0 0.9 %copy-start.2 = (s32[1,256,256]{2,1,0:T(8,128)S(1)}, s32[1,256,256]{2,1,0:T(8,128)}, u32[]{:S(2)}) copy-start(s32[1,256,256]{2,1,0:T(8,128)} %param.11) | copy-start | bytes 786436
  1.9 0.9 %copy-start.3 = (f32[1,256,256]{2,1,0:T(8,128)S(1)}, f32[1,256,256]{2,1,0:T(8,128)}, u32[]{:S(2)}) copy-start(f32[1,256,256]{2,1,0:T(8,128)} %param.12) | copy-start | bytes 786436
  2.9 0.9 %copy-start.4 = (f32[512,64]{1,0:T(8,128)S(1)}, f32[512,64]{1,0:T(8,128)}, u32[]{:S(2)}) copy-start(f32[512,64]{1,0:T(8,128)} %constant.5.clone.turns_ref) | copy-start | bytes 393220
  3.8 0.9 %copy-start.5 = (f32[512,128]{1,0:T(8,128)S(1)}, f32[512,128]{1,0:T(8,128)}, u32[]{:S(2)}) copy-start(f32[512,128]{1,0:T(8,128)} %constant.4.clone.spectrum_ref) | copy-start | bytes 786436
  4.8 0.7 %copy-start.7 = (s32[1,256,1]{1,2,0:T(1,128)S(1)}, s32[1,256,1]{1,2,0:T(1,128)}, u32[]{:S(2)}) copy-start(s32[1,256,1]{1,2,0:T(1,128)} %param.13) | copy-start | bytes 3076
  5.4 0.7 %copy-start.8 = (s32[1,256]{1,0:T(1,128)S(1)}, s32[1,256]{1,0:T(1,128)}, u32[]{:S(2)}) copy-start(s32[1,256]{1,0:T(1,128)} %shell_ref.1) | copy-start | bytes 3076
  6.1 0.7 %copy-start.9 = (s32[1,256]{1,0:T(1,128)S(1)}, s32[1,256]{1,0:T(1,128)}, u32[]{:S(2)}) copy-start(s32[1,256]{1,0:T(1,128)} %place_ref.1) | copy-start | bytes 3076
  15.5 1.6 %copy-start = (bf16[32,8,4096]{2,1,0:T(8,128)(2,1)S(1)}, bf16[32,8,4096]{2,1,0:T(8,128)(2,1)}, u32[]{:S(2)}) copy-start(bf16[32,8,4096]{2,1,0:T(8,128)(2,1)} %param.16) | copy-start | bytes 6291460
  17.2 0.7 %copy-start.6 = (f32[4,4]{1,0:T(4,128)S(1)}, f32[4,4]{1,0:T(4,128)}, u32[]{:S(2)}) copy-start(f32[4,4]{1,0:T(4,128)} %weight_ref.1) | copy-start | bytes 196

commit v2 on v1

--- a/solution.py
+++ b/solution.py
@@ -36,13 +36,14 @@
     return spectrum, turns
 
 
-def deposit_kernel(
+def deposit(
     sky_count, owners, cycle_ref, pixel_ref, mass_ref, block_ref, shell_ref, place_ref, spectrum_ref,
-    turns_ref, out_ref, pixel_t, mass0_t, mass1_t, hist_ref,
+    turns_ref, out_ref, pixel_t, mass0_t, mass1_t, hist_ref, fetch_particles, fetch_tables, early,
 ):
     tiles, particles = pixel_ref.shape
     lanes = 128
     rows = 64
+    fetch_particles()
     masses = mass_ref[...]
     first = cycle_ref[...] == 0
     for held, value in (
@@ -66,8 +67,11 @@
 
             zero = jnp.zeros((rows, lanes), jnp.float32)
             one, two = lax.fori_loop(0, particles, step, (zero, zero), unroll=8)
+            if side == 0 and top == 0:
+                early()
             hist_ref[0, top : top + rows, columns] = one
             hist_ref[1, top : top + rows, columns] = two
+    fetch_tables()
     position = (
         lax.broadcasted_iota(jnp.int32, (NBLK, tiles), 0) == place_ref[...]
     ).astype(jnp.float32)
@@ -97,10 +101,31 @@
         out_ref[z] = binned[:, z * width : (z + 1) * width]
 
 
-def mode_kernel(
-    counts, per, blocks, cycles, weight_ref, parts_ref, basis_ref, out_ref,
-    halves, arrived, own_sem, half_send, half_recv, part_send, part_recv,
+def kernel(
+    counts, per, blocks, cycles, cycle_hbm, pixel_hbm, mass_hbm, block_hbm, shell_hbm, place_hbm,
+    spectrum_hbm, turns_hbm, weight_hbm, basis_ref, out_ref,
+    cycle_ref, pixel_ref, mass_ref, block_ref, shell_ref, place_ref, spectrum_ref, turns_ref,
+    weight_ref, pixel_t, mass0_t, mass1_t, hist_ref, parts_ref,
+    halves, arrived, fetch_sem, own_sem, half_send, half_recv, part_send, part_recv,
 ):
+    fetches = [
+        pltpu.make_async_copy(source, target, fetch_sem.at[n])
+        for n, (source, target) in enumerate(
+            (
+                (cycle_hbm, cycle_ref),
+                (pixel_hbm, pixel_ref),
+                (mass_hbm, mass_ref),
+                (spectrum_hbm, spectrum_ref),
+                (turns_hbm, turns_ref),
+                (block_hbm, block_ref),
+                (shell_hbm, shell_ref),
+                (place_hbm, place_ref),
+                (weight_hbm, weight_ref),
+            )
+        )
+    ]
+    for fetch in fetches:
+        fetch.start()
     shell_count, sky_count, sub_count = counts
     shell, sky, sub = lax.axis_index("shell"), lax.axis_index("sky"), lax.axis_index("sub")
     peers = shell_count * sky_count * sub_count
@@ -122,8 +147,6 @@
         pl.semaphore_signal(
             barrier, inc=1, device_id=place((me + j) % peers), device_id_type=MESH
         )
-
-    pl.semaphore_wait(barrier, peers - 1)
 
     def send(j):
         target = place((me + j) % peers)
@@ -147,10 +170,6 @@
             device_id_type=MESH,
         )
 
-    @pl.loop(1, peers)
-    def _(j):
-        send(j).start()
-
     def half(j):
         target = (sub + j) % sub_count
         return pltpu.make_async_remote_copy(
@@ -173,14 +192,36 @@
             device_id_type=MESH,
         )
 
-    for j in range(1, sub_count):
-        half(j).start()
     own = pltpu.make_async_copy(
         basis_ref.at[:, pl.ds(pl.multiple_of(sub * degrees, degrees), degrees)],
         halves.at[sub],
         own_sem,
     )
     own.start()
+
+    def fetch_particles():
+        for fetch in fetches[:3]:
+            fetch.wait()
+
+    def fetch_tables():
+        for fetch in fetches[3:]:
+            fetch.wait()
+
+    def early():
+        pl.semaphore_wait(barrier, peers - 1)
+        for j in range(1, sub_count):
+            half(j).start()
+
+    deposit(
+        sky_count, blocks, cycle_ref, pixel_ref, mass_ref, block_ref, shell_ref, place_ref,
+        spectrum_ref, turns_ref, parts_ref, pixel_t, mass0_t, mass1_t, hist_ref,
+        fetch_particles, fetch_tables, early,
+    )
+
+    @pl.loop(1, peers)
+    def _(j):
+        send(j).start()
+
     arrived[me] = parts_ref[sky]
 
     @pl.loop(1, peers)
@@ -266,20 +307,39 @@
     bins = SHELL_DEV * owners
     width = 2 * CYCLE_DEV * orders
     spectrum, turns = tables()
-    vmem = pl.BlockSpec(memory_space=pltpu.VMEM)
-    parts = pl.pallas_call(
-        functools.partial(deposit_kernel, sky_count, owners),
-        out_shape=jax.ShapeDtypeStruct((sky_count, bins, width), jnp.float32),
-        in_specs=[vmem] * 8,
-        out_specs=vmem,
+    result = pl.pallas_call(
+        functools.partial(kernel, (shell_count, sky_count, sub_count), per, owners, cycles),
+        out_shape=jax.ShapeDtypeStruct((per, 2 * orders, share), jnp.float32),
+        in_specs=[pl.BlockSpec(memory_space=pltpu.HBM)] * 10,
+        out_specs=pl.BlockSpec(memory_space=pltpu.VMEM),
         scratch_shapes=[
+            pltpu.VMEM((tiles, particles), jnp.int32),
+            pltpu.VMEM((tiles, particles), jnp.int32),
+            pltpu.VMEM((tiles, particles), jnp.float32),
+            pltpu.VMEM((1, tiles), jnp.int32),
+            pltpu.VMEM((1, tiles), jnp.int32),
+            pltpu.VMEM((1, tiles), jnp.int32),
+            pltpu.VMEM(spectrum.shape, jnp.float32),
+            pltpu.VMEM(turns.shape, jnp.float32),
+            pltpu.SMEM(lens_weight.shape, jnp.float32),
             pltpu.VMEM((tiles // 128, particles, 128), jnp.int32),
             pltpu.VMEM((tiles // 128, particles, 128), jnp.float32),
             pltpu.VMEM((tiles // 128, particles, 128), jnp.float32),
             pltpu.VMEM((CYCLE_DEV, TP, tiles), jnp.float32),
+            pltpu.VMEM((sky_count, bins, width), jnp.float32),
+            pltpu.VMEM((sub_count, orders * cycles, share), jnp.bfloat16),
+            pltpu.VMEM((peers, bins, width), jnp.float32),
+            pltpu.SemaphoreType.DMA((9,)),
+            pltpu.SemaphoreType.DMA,
+            pltpu.SemaphoreType.DMA((sub_count,)),
+            pltpu.SemaphoreType.DMA((sub_count,)),
+            pltpu.SemaphoreType.DMA((peers,)),
+            pltpu.SemaphoreType.DMA((peers,)),
         ],
-        compiler_params=pltpu.CompilerParams(vmem_limit_bytes=24 << 20),
-        name="deposit",
+        compiler_params=pltpu.CompilerParams(
+            collective_id=0, has_side_effects=True, vmem_limit_bytes=60 << 20
+        ),
+        name="modes",
     )(
         part_cycle[0],
         part_pixel[0],
@@ -289,26 +349,9 @@
         tile_pixel,
         spectrum,
         turns,
-    )
-    result = pl.pallas_call(
-        functools.partial(mode_kernel, (shell_count, sky_count, sub_count), per, owners, cycles),
-        out_shape=jax.ShapeDtypeStruct((per, 2 * orders, share), jnp.float32),
-        in_specs=[pl.BlockSpec(memory_space=pltpu.SMEM), vmem, pl.BlockSpec(memory_space=pl.ANY)],
-        out_specs=vmem,
-        scratch_shapes=[
-            pltpu.VMEM((sub_count, orders * cycles, share), jnp.bfloat16),
-            pltpu.VMEM((peers, bins, width), jnp.float32),
-            pltpu.SemaphoreType.DMA,
-            pltpu.SemaphoreType.DMA((sub_count,)),
-            pltpu.SemaphoreType.DMA((sub_count,)),
-            pltpu.SemaphoreType.DMA((peers,)),
-            pltpu.SemaphoreType.DMA((peers,)),
-        ],
-        compiler_params=pltpu.CompilerParams(
-            collective_id=0, has_side_effects=True, vmem_limit_bytes=24 << 20
-        ),
-        name="modes",
-    )(lens_weight, parts, harmonic_basis.reshape(orders * cycles, degrees))
+        lens_weight,
+        harmonic_basis.reshape(orders * cycles, degrees),
+    )
     return result.reshape(per, orders, 2, share)
 
 

time: 32.1 us -> 23.1 us (0.72)
  local copies, waits for them, and re-layouts: 10.7 us -> 2.81 us
  Pallas kernels: 21 us -> 20.1 us
    unnamed x20 -> x0, local copies, waits for them, and re-layouts: 9.09 us -> none
    reshape x1, local copies, waits for them, and re-layouts: 1.59 us -> 2.81 us  [body(): return result.reshape(per, orders, 2, share)]
    pallas_call x2 -> x1, Pallas kernels: 21 us -> 20.1 us  [body(): pl.pallas_call(functools.partial(kernel, (shell_count, sky_count, sub_cou...]
where the time goes in v2:
time: 23.1 us; the launch traced here: 23 us
  Pallas kernels  20.1 us (87%)
  local copies, waits for them, and re-layouts  2.81 us (12%)
    pallas_call x1, Pallas kernels, body(): pl.pallas_call(functools.partial(kernel, (shell_count, sky_count, sub_cou...  20.1 us
    reshape x1, local copies, waits for them, and re-layouts, body(): return result.reshape(per, orders, 2, share)  2.81 us

profile of v2, /device:TPU:0, one launch (start us, length us, event | category | flops | bytes accessed | tf_op | source)
XLA Modules:
  0.0 23.0 jit_solution(4456862328603142481)
XLA Ops:
  0.0 20.1 %modes.1 = f32[2,64,2048]{2,1,0:T(8,128)} custom-call(s32[256,256]{1,0:T(8,128)} %bitcast.6, s32[256,256]{1,0:T(8,128)} %bitcast.7, f32[256,256]{1,0:T(8,128)} %bitcast.8, s32[1,256]{1,0:T(1,128)} %bitcast.9, s32[1,256]{1,0:T(1,128)} %shell_hbm.1, s32[1,256]{1,0:T(1,128)} %place_hbm.1, f32[512,128]{1,0:T(8,128)} %constant.4.clone.spectrum_hbm, ...), custom_call_target="tpu_custom_call" | custom-call | tf_op jit(solution)/shard_map/modes/pallas_call | solution.py:310
  20.2 2.8 %reshape.11 = f32[2,32,2,2048]{3,2,1,0:T(2,128)} reshape(f32[2,64,2048]{2,1,0:T(8,128)} %modes.1) | data formatting | bytes 2097152 | tf_op jit(solution)/shard_map/reshape | solution.py:355

commit v3 on v2

--- a/solution.py
+++ b/solution.py
@@ -16,7 +16,6 @@
 SHELL_DEV = 2
 NBLK = NP // TP
 
-precise = lax.Precision.HIGHEST
 MESH = pl.DeviceIdType.MESH
 
 
@@ -25,96 +24,163 @@
     smooth = np.exp(-((pixel[:, None] - pixel[None, :]) ** 2) / 18.0)
     orders = np.arange(M)
     angle = 2.0 * math.pi * ((np.arange(TP)[:, None] * orders[None, :]) % NP) / NP
-    real, imag = smooth @ np.cos(angle), -(smooth @ np.sin(angle))
-    straight = np.stack([real, imag], axis=2).reshape(TP, 2 * M).T
-    crossed = np.stack([-imag, real], axis=2).reshape(TP, 2 * M).T
     turn = 2.0 * math.pi * ((np.arange(NBLK)[:, None] * TP * orders[None, :]) % NP) / NP
-    cosine = np.repeat(np.cos(turn), 2, axis=1).T
-    sine = np.repeat(-np.sin(turn), 2, axis=1).T
-    spectrum = np.concatenate([straight, crossed], axis=0).astype(np.float32)
-    turns = np.concatenate([cosine, sine], axis=0).astype(np.float32)
-    return spectrum, turns
+    spectrum = np.concatenate([smooth @ np.cos(angle), -(smooth @ np.sin(angle))], axis=1)
+    turns = np.concatenate([np.cos(turn), -np.sin(turn)], axis=1)
+
+    def split(table):
+        high = table.astype(jnp.bfloat16)
+        low = (table - high.astype(np.float64)).astype(jnp.bfloat16)
+        return np.concatenate([high, low], axis=0).astype(np.float32)
+
+    return split(spectrum), split(turns)
+
+
+def split(values):
+    high = values.astype(jnp.bfloat16)
+    return high, (values - high.astype(jnp.float32)).astype(jnp.bfloat16)
+
+
+def dot(one, two, right=0):
+    return lax.dot_general(
+        one, two, (((1,), (right,)), ((), ())), preferred_element_type=jnp.float32
+    )
+
+
+FINE = 32
+SIDE = 128
 
 
 def deposit(
     sky_count, owners, cycle_ref, pixel_ref, mass_ref, block_ref, shell_ref, place_ref, spectrum_ref,
-    turns_ref, out_ref, pixel_t, mass0_t, mass1_t, hist_ref, fetch_particles, fetch_tables, early,
+    turns_ref, out_ref, key_ref, fine_ref, high_ref, low_ref, hist_ref, fetch_particles, fetch_tables,
+    early,
 ):
-    tiles, particles = pixel_ref.shape
-    lanes = 128
-    rows = 64
+    halves, tiles = pixel_ref.shape[:2]
+    coarse = TP // FINE
+    bundle = 2 * SIDE // FINE
+    groups = tiles // bundle
+    keys = CYCLE_DEV * coarse
     fetch_particles()
     masses = mass_ref[...]
-    first = cycle_ref[...] == 0
-    for held, value in (
-        (pixel_t, pixel_ref[...]),
-        (mass0_t, jnp.where(first, masses, 0.0)),
-        (mass1_t, jnp.where(first, 0.0, masses)),
-    ):
-        turned = value.T
-        for side in range(tiles // lanes):
-            held[side] = turned[:, side * lanes : (side + 1) * lanes]
-    for side in range(tiles // lanes):
-        columns = slice(side * lanes, (side + 1) * lanes)
-        for top in range(0, TP, rows):
-            ids = lax.broadcasted_iota(jnp.int32, (rows, lanes), 0) + top
-
-            def step(p, sums):
-                here = jnp.broadcast_to(pixel_t[side, pl.ds(p, 1), :], (rows, lanes)) == ids
-                one = jnp.broadcast_to(mass0_t[side, pl.ds(p, 1), :], (rows, lanes))
-                two = jnp.broadcast_to(mass1_t[side, pl.ds(p, 1), :], (rows, lanes))
-                return sums[0] + jnp.where(here, one, 0.0), sums[1] + jnp.where(here, two, 0.0)
-
-            zero = jnp.zeros((rows, lanes), jnp.float32)
-            one, two = lax.fori_loop(0, particles, step, (zero, zero), unroll=8)
-            if side == 0 and top == 0:
-                early()
-            hist_ref[0, top : top + rows, columns] = one
-            hist_ref[1, top : top + rows, columns] = two
+    pixels = pixel_ref[...]
+    high = masses.astype(jnp.bfloat16).astype(jnp.float32)
+    high_ref[...] = high
+    low_ref[...] = masses - high
+    fine_ref[...] = pixels % FINE
+    key_ref[...] = cycle_ref[...] * coarse + pixels // FINE
+    fine_ids = lax.broadcasted_iota(jnp.int32, (FINE, SIDE), 0)
+    key_ids = lax.broadcasted_iota(jnp.int32, (keys, SIDE), 0)
+    same = (
+        lax.broadcasted_iota(jnp.int32, (bundle * keys, bundle * FINE), 0) // keys
+        == lax.broadcasted_iota(jnp.int32, (bundle * keys, bundle * FINE), 1) // FINE
+    )
+
+    def group(g, carry):
+        spread, highs, lows = [], [], []
+        for t in range(bundle):
+            row = pl.ds(t * groups + g, 1)
+            spread_t, high_t, low_t = [], [], []
+            for h in range(halves):
+                fine = jnp.broadcast_to(fine_ref[h, row, :], (FINE, SIDE))
+                spread_t.append(jnp.where(fine == fine_ids, 1.0, 0.0))
+                here = jnp.broadcast_to(key_ref[h, row, :], (keys, SIDE)) == key_ids
+                high_t.append(
+                    jnp.where(here, jnp.broadcast_to(high_ref[h, row, :], (keys, SIDE)), 0.0)
+                )
+                low_t.append(
+                    jnp.where(here, jnp.broadcast_to(low_ref[h, row, :], (keys, SIDE)), 0.0)
+                )
+            spread.append(jnp.concatenate(spread_t, axis=1).astype(jnp.bfloat16))
+            highs.append(jnp.concatenate(high_t, axis=1))
+            lows.append(jnp.concatenate(low_t, axis=1))
+        weights = jnp.concatenate(highs + lows, axis=0).astype(jnp.bfloat16)
+        pairs = dot(weights, jnp.concatenate(spread, axis=0), 1)
+        count = bundle * keys
+        pairs = jnp.where(same, pairs[:count] + pairs[count:], 0.0)
+        own = jnp.sum(pairs.reshape(bundle, keys, bundle * FINE), axis=0)
+        at = pl.ds(pl.multiple_of(g * keys, keys), keys)
+        for side in range(bundle * FINE // SIDE):
+            hist_ref[side, at, :] = own[:, side * SIDE : (side + 1) * SIDE]
+        return carry
+
+    lax.fori_loop(0, groups // 2, group, 0, unroll=4)
+    early()
+    lax.fori_loop(groups // 2, groups, group, 0, unroll=4)
     fetch_tables()
-    position = (
-        lax.broadcasted_iota(jnp.int32, (NBLK, tiles), 0) == place_ref[...]
-    ).astype(jnp.float32)
-    turns = jnp.dot(turns_ref[...], position, precision=precise, preferred_element_type=jnp.float32)
-    cosine, sine = turns[: 2 * M], turns[2 * M :]
-    near = math.exp(-0.5)
+    lane = lax.broadcasted_iota(jnp.int32, (groups, SIDE), 1) // FINE
+    strips = [
+        [hist_ref[side, pl.ds(key, groups, stride=keys), :] for key in range(keys)]
+        for side in range(bundle * FINE // SIDE)
+    ]
+    hist = []
+    for c in range(CYCLE_DEV):
+        for t in range(bundle):
+            side, offset = t * FINE // SIDE, t * FINE % SIDE
+            joined = None
+            for x in range(coarse):
+                shift = (x * FINE - offset) % SIDE
+                strip = strips[side][c * coarse + x]
+                moved = strip if shift == 0 else pltpu.roll(strip, shift, 1)
+                joined = moved if joined is None else jnp.where(lane == x, moved, joined)
+            hist.append(joined)
+    high, low = split(jnp.concatenate(hist, axis=0))
+    spectrum = spectrum_ref[...].astype(jnp.bfloat16)
+    modes = dot(high, spectrum[:TP]) + dot(low, spectrum[:TP]) + dot(high, spectrum[TP:])
+    position = lax.broadcasted_iota(jnp.int32, (2 * NBLK, tiles), 0) % NBLK == place_ref[...]
+    position = jnp.where(position, 1.0, 0.0).T.astype(jnp.bfloat16)
+    turns = dot(position, turns_ref[...].astype(jnp.bfloat16))
+    cosine, sine = turns[:, :M], turns[:, M:]
     turned = []
-    for k in range(CYCLE_DEV):
-        mixed = hist_ref[k] + near * hist_ref[1 - k]
-        modes = jnp.dot(
-            spectrum_ref[...], mixed, precision=precise, preferred_element_type=jnp.float32
-        )
-        turned.append(modes[: 2 * M] * cosine + modes[2 * M :] * sine)
-    share = 2 * M // sky_count
-    stacked = jnp.concatenate(
-        [turned[k][z * share : (z + 1) * share] for z in range(sky_count) for k in range(CYCLE_DEV)],
-        axis=0,
-    )
+    for c in range(CYCLE_DEV):
+        real = modes[c * tiles : (c + 1) * tiles, :M]
+        imag = modes[c * tiles : (c + 1) * tiles, M:]
+        turned += [real * cosine - imag * sine, real * sine + imag * cosine]
     bins = SHELL_DEV * owners
     key = shell_ref[...] * owners + block_ref[...]
-    hot = (lax.broadcasted_iota(jnp.int32, (bins, tiles), 0) == key).astype(jnp.float32)
-    binned = lax.dot_general(
-        hot, stacked, (((1,), (1,)), ((), ())), precision=precise, preferred_element_type=jnp.float32
-    )
-    width = CYCLE_DEV * share
+    hot = lax.broadcasted_iota(jnp.int32, (bins, tiles), 0) == key
+    hot = jnp.where(hot, 1.0, 0.0).astype(jnp.bfloat16)
+    high, low = split(jnp.concatenate(turned, axis=1))
+    binned = dot(hot, high) + dot(hot, low)
+    pieces = [binned[:, n * M : (n + 1) * M] for n in range(2 * CYCLE_DEV)]
+    near = math.exp(-0.5)
+    pieces = [
+        pieces[2 * k + part] + near * pieces[2 * (1 - k) + part]
+        for k in range(CYCLE_DEV)
+        for part in range(2)
+    ]
+    share = M // sky_count
+    width = len(pieces) * share
+    lane = lax.broadcasted_iota(jnp.int32, (bins, M), 1) // share
     for z in range(sky_count):
-        out_ref[z] = binned[:, z * width : (z + 1) * width]
+        message = None
+        for n, piece in enumerate(pieces):
+            shift = (n - z) * share % M
+            moved = piece if shift == 0 else pltpu.roll(piece, shift, 1)
+            message = moved if message is None else jnp.where(lane == n, moved, message)
+        out_ref[z] = message[:, :width]
 
 
 def kernel(
     counts, per, blocks, cycles, cycle_hbm, pixel_hbm, mass_hbm, block_hbm, shell_hbm, place_hbm,
     spectrum_hbm, turns_hbm, weight_hbm, basis_ref, out_ref,
     cycle_ref, pixel_ref, mass_ref, block_ref, shell_ref, place_ref, spectrum_ref, turns_ref,
-    weight_ref, pixel_t, mass0_t, mass1_t, hist_ref, parts_ref,
+    weight_ref, key_ref, fine_ref, high_ref, low_ref, hist_ref, parts_ref,
     halves, arrived, fetch_sem, own_sem, half_send, half_recv, part_send, part_recv,
 ):
     fetches = [
         pltpu.make_async_copy(source, target, fetch_sem.at[n])
         for n, (source, target) in enumerate(
             (
-                (cycle_hbm, cycle_ref),
-                (pixel_hbm, pixel_ref),
-                (mass_hbm, mass_ref),
+                *(
+                    (array.at[:, h * SIDE : (h + 1) * SIDE], held.at[h])
+                    for array, held in (
+                        (cycle_hbm, cycle_ref),
+                        (pixel_hbm, pixel_ref),
+                        (mass_hbm, mass_ref),
+                    )
+                    for h in range(cycle_ref.shape[0])
+                ),
                 (spectrum_hbm, spectrum_ref),
                 (turns_hbm, turns_ref),
                 (block_hbm, block_ref),
@@ -200,11 +266,11 @@
     own.start()
 
     def fetch_particles():
-        for fetch in fetches[:3]:
+        for fetch in fetches[:-6]:
             fetch.wait()
 
     def fetch_tables():
-        for fetch in fetches[3:]:
+        for fetch in fetches[-6:]:
             fetch.wait()
 
     def early():
@@ -214,7 +280,7 @@
 
     deposit(
         sky_count, blocks, cycle_ref, pixel_ref, mass_ref, block_ref, shell_ref, place_ref,
-        spectrum_ref, turns_ref, parts_ref, pixel_t, mass0_t, mass1_t, hist_ref,
+        spectrum_ref, turns_ref, parts_ref, key_ref, fine_ref, high_ref, low_ref, hist_ref,
         fetch_particles, fetch_tables, early,
     )
 
@@ -241,24 +307,28 @@
                 weight = jnp.where(lens <= source, weight_ref[source, lens], 0.0)
                 term = weight * part
                 folded[i] = term if folded[i] is None else folded[i] + term
-    coefficients = jnp.concatenate(folded, axis=0).T
-    high = coefficients.astype(jnp.bfloat16)
-    low = (coefficients - high.astype(jnp.float32)).astype(jnp.bfloat16)
+    folded = jnp.concatenate(split(jnp.concatenate(folded, axis=0)), axis=0)
+    width = folded.shape[1]
+    to = lax.broadcasted_iota(jnp.int32, (width, width), 0)
+    source = to // (2 * orders) * (2 * orders) + to % 2 * orders + to % (2 * orders) // 2
+    swap = source == lax.broadcasted_iota(jnp.int32, (width, width), 1)
+    swap = jnp.where(swap, 1.0, 0.0).astype(jnp.bfloat16)
+    coefficients = dot(swap, folded, 1).astype(jnp.bfloat16)
     depth = orders * cycles
     span = 2 * orders
-    lane = lax.broadcasted_iota(jnp.int32, (per * blocks, depth), 1)
-    row = lax.broadcasted_iota(jnp.int32, (per * blocks, depth), 0)
+    lane = lax.broadcasted_iota(jnp.int32, (2 * per * blocks, depth), 1)
+    row = lax.broadcasted_iota(jnp.int32, (2 * per * blocks, depth), 0)
     lane_out = lax.broadcasted_iota(jnp.int32, (span, depth), 1)
     diagonal = lane_out // cycles == lax.broadcasted_iota(jnp.int32, (span, depth), 0) // 2
     even = lane_out % CYCLE_DEV == 0
     left = []
     for h in range(sub_count):
         rows = []
-        for piece in (high, low):
+        for piece in range(2):
             for i in range(per):
-                block = i * blocks + h * (cycles // CYCLE_DEV) + lane % cycles // CYCLE_DEV
-                pick = (row == block).astype(jnp.float32).astype(jnp.bfloat16)
-                spread = jnp.dot(piece, pick, preferred_element_type=jnp.float32)
+                block = (piece * per + i) * blocks + h * (cycles // CYCLE_DEV) + lane % cycles // CYCLE_DEV
+                pick = jnp.where(row == block, 1.0, 0.0).astype(jnp.bfloat16)
+                spread = dot(coefficients, pick)
                 chosen = jnp.where(even, spread[:span], spread[span:])
                 rows.append(jnp.where(diagonal, chosen, 0.0).astype(jnp.bfloat16))
         left.append(jnp.concatenate(rows, axis=0))
@@ -274,7 +344,7 @@
             result = term if result is None else result + term
         result = result[: per * span] + result[per * span :]
         for i in range(per):
-            out_ref[i, :, columns] = result[i * span : (i + 1) * span]
+            out_ref[i, :, :, columns] = result[i * span : (i + 1) * span].reshape(orders, 2, step)
     for j in range(1, sub_count):
         half(j).wait_send()
 
@@ -309,27 +379,28 @@
     spectrum, turns = tables()
     result = pl.pallas_call(
         functools.partial(kernel, (shell_count, sky_count, sub_count), per, owners, cycles),
-        out_shape=jax.ShapeDtypeStruct((per, 2 * orders, share), jnp.float32),
+        out_shape=pltpu.VMEM((per, orders, 2, share), jnp.float32),
         in_specs=[pl.BlockSpec(memory_space=pltpu.HBM)] * 10,
         out_specs=pl.BlockSpec(memory_space=pltpu.VMEM),
         scratch_shapes=[
-            pltpu.VMEM((tiles, particles), jnp.int32),
-            pltpu.VMEM((tiles, particles), jnp.int32),
-            pltpu.VMEM((tiles, particles), jnp.float32),
+            pltpu.VMEM((particles // SIDE, tiles, SIDE), jnp.int32),
+            pltpu.VMEM((particles // SIDE, tiles, SIDE), jnp.int32),
+            pltpu.VMEM((particles // SIDE, tiles, SIDE), jnp.float32),
             pltpu.VMEM((1, tiles), jnp.int32),
             pltpu.VMEM((1, tiles), jnp.int32),
             pltpu.VMEM((1, tiles), jnp.int32),
             pltpu.VMEM(spectrum.shape, jnp.float32),
             pltpu.VMEM(turns.shape, jnp.float32),
             pltpu.SMEM(lens_weight.shape, jnp.float32),
-            pltpu.VMEM((tiles // 128, particles, 128), jnp.int32),
-            pltpu.VMEM((tiles // 128, particles, 128), jnp.float32),
-            pltpu.VMEM((tiles // 128, particles, 128), jnp.float32),
-            pltpu.VMEM((CYCLE_DEV, TP, tiles), jnp.float32),
+            pltpu.VMEM((particles // SIDE, tiles, SIDE), jnp.int32),
+            pltpu.VMEM((particles // SIDE, tiles, SIDE), jnp.int32),
+            pltpu.VMEM((particles // SIDE, tiles, SIDE), jnp.float32),
+            pltpu.VMEM((particles // SIDE, tiles, SIDE), jnp.float32),
+            pltpu.VMEM((2, tiles * CYCLE_DEV * TP // (2 * SIDE), SIDE), jnp.float32),
             pltpu.VMEM((sky_count, bins, width), jnp.float32),
             pltpu.VMEM((sub_count, orders * cycles, share), jnp.bfloat16),
             pltpu.VMEM((peers, bins, width), jnp.float32),
-            pltpu.SemaphoreType.DMA((9,)),
+            pltpu.SemaphoreType.DMA((3 * (particles // SIDE) + 6,)),
             pltpu.SemaphoreType.DMA,
             pltpu.SemaphoreType.DMA((sub_count,)),
             pltpu.SemaphoreType.DMA((sub_count,)),
@@ -352,7 +423,7 @@
         lens_weight,
         harmonic_basis.reshape(orders * cycles, degrees),
     )
-    return result.reshape(per, orders, 2, share)
+    return result
 
 
 def solution(mesh):

time: 23.1 us -> 15.7 us (0.68)
  Pallas kernels: 20.1 us -> 14.5 us
  local copies, waits for them, and re-layouts: 2.81 us -> 0.97 us
    pallas_call x1, Pallas kernels: 20.1 us -> 14.5 us  [body(): pl.pallas_call(functools.partial(kernel, (shell_count, sky_count, sub_cou...]
    reshape x1 -> x0, local copies, waits for them, and re-layouts: 2.81 us -> none  [body(): return result.reshape(per, orders, 2, share)]
    unnamed x0 -> x1, local copies, waits for them, and re-layouts: none -> 0.97 us
where the time goes in v3:
time: 15.7 us; the launch traced here: 15.5 us
  Pallas kernels  14.5 us (92%)
  local copies, waits for them, and re-layouts  0.97 us (6%)
    pallas_call x1, Pallas kernels, body(): pl.pallas_call(functools.partial(kernel, (shell_count, sky_count, sub_cou...  14.5 us
    unnamed x1, local copies, waits for them, and re-layouts  0.97 us

profile of v3, /device:TPU:0, one launch (start us, length us, event | category | flops | bytes accessed | tf_op | source)
XLA Modules:
  0.0 15.5 jit_solution(15283038636193764006)
XLA Ops:
  0.0 14.5 %modes.1 = f32[2,32,2,2048]{3,2,1,0:T(2,128)S(1)} custom-call(s32[256,256]{1,0:T(8,128)} %bitcast.6, s32[256,256]{1,0:T(8,128)} %bitcast.7, f32[256,256]{1,0:T(8,128)} %bitcast.8, s32[1,256]{1,0:T(1,128)} %bitcast.9, s32[1,256]{1,0:T(1,128)} %shell_hbm.1, s32[1,256]{1,0:T(1,128)} %place_hbm.1, f32[256,256]{1,0:T(8,128)} %constant.4.clone.spectrum_hbm, ...), custom_call_target="tpu_custom_call" | custom-call | tf_op jit(solution)/shard_map/modes/pallas_call | solution.py:380
  14.5 1.0 %copy.12 = f32[2,32,2,2048]{3,2,1,0:T(2,128)} copy(f32[2,32,2,2048]{3,2,1,0:T(2,128)S(1)} %modes.1) | data formatting | bytes 2097152

commit v4 on v3

--- a/solution.py
+++ b/solution.py
@@ -49,6 +49,14 @@
 
 FINE = 32
 SIDE = 128
+
+
+def quotient(value, by):
+    return value >> (by.bit_length() - 1) if by & (by - 1) == 0 else value // by
+
+
+def rest(value, by):
+    return value & (by - 1) if by & (by - 1) == 0 else value % by
 
 
 def deposit(
@@ -67,13 +75,13 @@
     high = masses.astype(jnp.bfloat16).astype(jnp.float32)
     high_ref[...] = high
     low_ref[...] = masses - high
-    fine_ref[...] = pixels % FINE
-    key_ref[...] = cycle_ref[...] * coarse + pixels // FINE
+    fine_ref[...] = rest(pixels, FINE)
+    key_ref[...] = cycle_ref[...] * coarse + quotient(pixels, FINE)
     fine_ids = lax.broadcasted_iota(jnp.int32, (FINE, SIDE), 0)
     key_ids = lax.broadcasted_iota(jnp.int32, (keys, SIDE), 0)
     same = (
-        lax.broadcasted_iota(jnp.int32, (bundle * keys, bundle * FINE), 0) // keys
-        == lax.broadcasted_iota(jnp.int32, (bundle * keys, bundle * FINE), 1) // FINE
+        quotient(lax.broadcasted_iota(jnp.int32, (bundle * keys, bundle * FINE), 0), keys)
+        == quotient(lax.broadcasted_iota(jnp.int32, (bundle * keys, bundle * FINE), 1), FINE)
     )
 
     def group(g, carry):
@@ -108,7 +116,7 @@
     early()
     lax.fori_loop(groups // 2, groups, group, 0, unroll=4)
     fetch_tables()
-    lane = lax.broadcasted_iota(jnp.int32, (groups, SIDE), 1) // FINE
+    lane = quotient(lax.broadcasted_iota(jnp.int32, (groups, SIDE), 1), FINE)
     strips = [
         [hist_ref[side, pl.ds(key, groups, stride=keys), :] for key in range(keys)]
         for side in range(bundle * FINE // SIDE)
@@ -127,7 +135,7 @@
     high, low = split(jnp.concatenate(hist, axis=0))
     spectrum = spectrum_ref[...].astype(jnp.bfloat16)
     modes = dot(high, spectrum[:TP]) + dot(low, spectrum[:TP]) + dot(high, spectrum[TP:])
-    position = lax.broadcasted_iota(jnp.int32, (2 * NBLK, tiles), 0) % NBLK == place_ref[...]
+    position = rest(lax.broadcasted_iota(jnp.int32, (2 * NBLK, tiles), 0), NBLK) == place_ref[...]
     position = jnp.where(position, 1.0, 0.0).T.astype(jnp.bfloat16)
     turns = dot(position, turns_ref[...].astype(jnp.bfloat16))
     cosine, sine = turns[:, :M], turns[:, M:]
@@ -151,7 +159,7 @@
     ]
     share = M // sky_count
     width = len(pieces) * share
-    lane = lax.broadcasted_iota(jnp.int32, (bins, M), 1) // share
+    lane = quotient(lax.broadcasted_iota(jnp.int32, (bins, M), 1), share)
     for z in range(sky_count):
         message = None
         for n, piece in enumerate(pieces):
@@ -201,21 +209,21 @@
 
     def place(rank):
         return dict(
-            shell=rank // (sky_count * sub_count),
-            sky=rank // sub_count % sky_count,
-            sub=rank % sub_count,
+            shell=quotient(rank, sky_count * sub_count),
+            sky=rest(quotient(rank, sub_count), sky_count),
+            sub=rest(rank, sub_count),
         )
 
     barrier = pltpu.get_barrier_semaphore()
 
-    @pl.loop(1, peers)
+    @pl.loop(1, peers, unroll=peers <= 16)
     def _(j):
         pl.semaphore_signal(
-            barrier, inc=1, device_id=place((me + j) % peers), device_id_type=MESH
+            barrier, inc=1, device_id=place(rest(me + j, peers)), device_id_type=MESH
         )
 
     def send(j):
-        target = place((me + j) % peers)
+        target = place(rest(me + j, peers))
         return pltpu.make_async_remote_copy(
             src_ref=parts_ref.at[target["sky"]],
             dst_ref=arrived.at[me],
@@ -226,7 +234,7 @@
         )
 
     def expect(j):
-        source = (me + peers - j) % peers
+        source = rest(me + peers - j, peers)
         return pltpu.make_async_remote_copy(
             src_ref=parts_ref.at[0],
             dst_ref=arrived.at[source],
@@ -237,7 +245,7 @@
         )
 
     def half(j):
-        target = (sub + j) % sub_count
+        target = rest(sub + j, sub_count)
         return pltpu.make_async_remote_copy(
             src_ref=basis_ref.at[:, pl.ds(pl.multiple_of(target * degrees, degrees), degrees)],
             dst_ref=halves.at[sub],
@@ -248,7 +256,7 @@
         )
 
     def expect_half(j):
-        source = (sub + sub_count - j) % sub_count
+        source = rest(sub + sub_count - j, sub_count)
         return pltpu.make_async_remote_copy(
             src_ref=basis_ref.at[:, pl.ds(0, degrees)],
             dst_ref=halves.at[source],
@@ -284,13 +292,13 @@
         fetch_particles, fetch_tables, early,
     )
 
-    @pl.loop(1, peers)
+    @pl.loop(1, peers, unroll=peers <= 16)
     def _(j):
         send(j).start()
 
     arrived[me] = parts_ref[sky]
 
-    @pl.loop(1, peers)
+    @pl.loop(1, peers, unroll=peers <= 16)
     def _(j):
         expect(j).wait_recv()
 
@@ -310,7 +318,8 @@
     folded = jnp.concatenate(split(jnp.concatenate(folded, axis=0)), axis=0)
     width = folded.shape[1]
     to = lax.broadcasted_iota(jnp.int32, (width, width), 0)
-    source = to // (2 * orders) * (2 * orders) + to % 2 * orders + to % (2 * orders) // 2
+    within = rest(to, 2 * orders)
+    source = to - within + rest(to, 2) * orders + quotient(within, 2)
     swap = source == lax.broadcasted_iota(jnp.int32, (width, width), 1)
     swap = jnp.where(swap, 1.0, 0.0).astype(jnp.bfloat16)
     coefficients = dot(swap, folded, 1).astype(jnp.bfloat16)
@@ -319,14 +328,17 @@
     lane = lax.broadcasted_iota(jnp.int32, (2 * per * blocks, depth), 1)
     row = lax.broadcasted_iota(jnp.int32, (2 * per * blocks, depth), 0)
     lane_out = lax.broadcasted_iota(jnp.int32, (span, depth), 1)
-    diagonal = lane_out // cycles == lax.broadcasted_iota(jnp.int32, (span, depth), 0) // 2
-    even = lane_out % CYCLE_DEV == 0
+    diagonal = quotient(lane_out, cycles) == quotient(
+        lax.broadcasted_iota(jnp.int32, (span, depth), 0), 2
+    )
+    even = rest(lane_out, CYCLE_DEV) == 0
+    turn = quotient(rest(lane, cycles), CYCLE_DEV)
     left = []
     for h in range(sub_count):
         rows = []
         for piece in range(2):
             for i in range(per):
-                block = (piece * per + i) * blocks + h * (cycles // CYCLE_DEV) + lane % cycles // CYCLE_DEV
+                block = (piece * per + i) * blocks + h * (cycles // CYCLE_DEV) + turn
                 pick = jnp.where(row == block, 1.0, 0.0).astype(jnp.bfloat16)
                 spread = dot(coefficients, pick)
                 chosen = jnp.where(even, spread[:span], spread[span:])
@@ -348,7 +360,7 @@
     for j in range(1, sub_count):
         half(j).wait_send()
 
-    @pl.loop(1, peers)
+    @pl.loop(1, peers, unroll=peers <= 16)
     def _(j):
         send(j).wait_send()
 

time: 15.7 us -> 15.3 us (0.975)
  Pallas kernels: 14.5 us -> 14.2 us
    pallas_call x1, Pallas kernels: 14.5 us -> 14.2 us  [body(): pl.pallas_call(functools.partial(kernel, (shell_count, sky_count, sub_cou...]
where the time goes in v4:
time: 15.3 us; the launch traced here: 15.2 us
  Pallas kernels  14.2 us (93%)
  local copies, waits for them, and re-layouts  0.97 us (6%)
    pallas_call x1, Pallas kernels, body(): pl.pallas_call(functools.partial(kernel, (shell_count, sky_count, sub_cou...  14.2 us
    unnamed x1, local copies, waits for them, and re-layouts  0.97 us

profile of v4, /device:TPU:0, one launch (start us, length us, event | category | flops | bytes accessed | tf_op | source)
XLA Modules:
  0.0 15.2 jit_solution(17031016924767655614)
XLA Ops:
  0.0 14.2 %modes.1 = f32[2,32,2,2048]{3,2,1,0:T(2,128)S(1)} custom-call(s32[256,256]{1,0:T(8,128)} %bitcast.6, s32[256,256]{1,0:T(8,128)} %bitcast.7, f32[256,256]{1,0:T(8,128)} %bitcast.8, s32[1,256]{1,0:T(1,128)} %bitcast.9, s32[1,256]{1,0:T(1,128)} %shell_hbm.1, s32[1,256]{1,0:T(1,128)} %place_hbm.1, f32[256,256]{1,0:T(8,128)} %constant.4.clone.spectrum_hbm, ...), custom_call_target="tpu_custom_call" | custom-call | tf_op jit(solution)/shard_map/modes/pallas_call | solution.py:392
  14.2 1.0 %copy.12 = f32[2,32,2,2048]{3,2,1,0:T(2,128)} copy(f32[2,32,2,2048]{3,2,1,0:T(2,128)S(1)} %modes.1) | data formatting | bytes 2097152

commit v5 on v4

--- a/solution.py
+++ b/solution.py
@@ -75,9 +75,11 @@
     high = masses.astype(jnp.bfloat16).astype(jnp.float32)
     high_ref[...] = high
     low_ref[...] = masses - high
-    fine_ref[...] = rest(pixels, FINE)
+    fine_ref[...] = rest(pixels, FINE).astype(jnp.float32)
     key_ref[...] = cycle_ref[...] * coarse + quotient(pixels, FINE)
     fine_ids = lax.broadcasted_iota(jnp.int32, (FINE, SIDE), 0)
+    fine_ids = fine_ids.astype(jnp.float32).astype(jnp.bfloat16)
+    ones, zeros = jnp.ones((FINE, SIDE), jnp.bfloat16), jnp.zeros((FINE, SIDE), jnp.bfloat16)
     key_ids = lax.broadcasted_iota(jnp.int32, (keys, SIDE), 0)
     same = (
         quotient(lax.broadcasted_iota(jnp.int32, (bundle * keys, bundle * FINE), 0), keys)
@@ -90,8 +92,8 @@
             row = pl.ds(t * groups + g, 1)
             spread_t, high_t, low_t = [], [], []
             for h in range(halves):
-                fine = jnp.broadcast_to(fine_ref[h, row, :], (FINE, SIDE))
-                spread_t.append(jnp.where(fine == fine_ids, 1.0, 0.0))
+                fine = jnp.broadcast_to(fine_ref[h, row, :], (FINE, SIDE)).astype(jnp.bfloat16)
+                spread_t.append(jnp.where(fine == fine_ids, ones, zeros))
                 here = jnp.broadcast_to(key_ref[h, row, :], (keys, SIDE)) == key_ids
                 high_t.append(
                     jnp.where(here, jnp.broadcast_to(high_ref[h, row, :], (keys, SIDE)), 0.0)
@@ -99,7 +101,7 @@
                 low_t.append(
                     jnp.where(here, jnp.broadcast_to(low_ref[h, row, :], (keys, SIDE)), 0.0)
                 )
-            spread.append(jnp.concatenate(spread_t, axis=1).astype(jnp.bfloat16))
+            spread.append(jnp.concatenate(spread_t, axis=1))
             highs.append(jnp.concatenate(high_t, axis=1))
             lows.append(jnp.concatenate(low_t, axis=1))
         weights = jnp.concatenate(highs + lows, axis=0).astype(jnp.bfloat16)
@@ -347,16 +349,19 @@
     own.wait()
     for j in range(1, sub_count):
         expect_half(j).wait_recv()
-    step = 512
-    for first in range(0, degrees, step):
-        columns = slice(first, first + step)
+    step = 256
+
+    @pl.loop(0, degrees // step)
+    def _(n):
+        columns = pl.ds(pl.multiple_of(n * step, step), step)
         result = None
         for h in range(sub_count):
-            term = jnp.dot(left[h], halves[h, :, columns], preferred_element_type=jnp.float32)
+            term = dot(left[h], halves[h, :, columns])
             result = term if result is None else result + term
         result = result[: per * span] + result[per * span :]
         for i in range(per):
             out_ref[i, :, :, columns] = result[i * span : (i + 1) * span].reshape(orders, 2, step)
+
     for j in range(1, sub_count):
         half(j).wait_send()
 
@@ -405,7 +410,7 @@
             pltpu.VMEM(turns.shape, jnp.float32),
             pltpu.SMEM(lens_weight.shape, jnp.float32),
             pltpu.VMEM((particles // SIDE, tiles, SIDE), jnp.int32),
-            pltpu.VMEM((particles // SIDE, tiles, SIDE), jnp.int32),
+            pltpu.VMEM((particles // SIDE, tiles, SIDE), jnp.float32),
             pltpu.VMEM((particles // SIDE, tiles, SIDE), jnp.float32),
             pltpu.VMEM((particles // SIDE, tiles, SIDE), jnp.float32),
             pltpu.VMEM((2, tiles * CYCLE_DEV * TP // (2 * SIDE), SIDE), jnp.float32),

time: 15.3 us -> 16.5 us (1.078)
  Pallas kernels: 14.2 us -> 15.4 us
    pallas_call x1, Pallas kernels: 14.2 us -> 15.4 us  [body(): pl.pallas_call(functools.partial(kernel, (shell_count, sky_count, sub_cou...]
where the time goes in v5:
time: 16.5 us; the launch traced here: 16.4 us
  Pallas kernels  15.4 us (93%)
  local copies, waits for them, and re-layouts  0.97 us (6%)
    pallas_call x1, Pallas kernels, body(): pl.pallas_call(functools.partial(kernel, (shell_count, sky_count, sub_cou...  15.4 us
    unnamed x1, local copies, waits for them, and re-layouts  0.97 us

profile of v5, /device:TPU:0, one launch (start us, length us, event | category | flops | bytes accessed | tf_op | source)
XLA Modules:
  0.0 16.4 jit_solution(16553367375874832866)
XLA Ops:
  0.0 15.4 %modes.1 = f32[2,32,2,2048]{3,2,1,0:T(2,128)S(1)} custom-call(s32[256,256]{1,0:T(8,128)} %bitcast.6, s32[256,256]{1,0:T(8,128)} %bitcast.7, f32[256,256]{1,0:T(8,128)} %bitcast.8, s32[1,256]{1,0:T(1,128)} %bitcast.9, s32[1,256]{1,0:T(1,128)} %shell_hbm.1, s32[1,256]{1,0:T(1,128)} %place_hbm.1, f32[256,256]{1,0:T(8,128)} %constant.4.clone.spectrum_hbm, ...), custom_call_target="tpu_custom_call" | custom-call | tf_op jit(solution)/shard_map/modes/pallas_call | solution.py:397
  15.4 1.0 %copy.12 = f32[2,32,2,2048]{3,2,1,0:T(2,128)} copy(f32[2,32,2,2048]{3,2,1,0:T(2,128)S(1)} %modes.1) | data formatting | bytes 2097152

commit v6 on v5

--- a/solution.py
+++ b/solution.py
@@ -114,9 +114,9 @@
             hist_ref[side, at, :] = own[:, side * SIDE : (side + 1) * SIDE]
         return carry
 
-    lax.fori_loop(0, groups // 2, group, 0, unroll=4)
+    lax.fori_loop(0, groups // 2, group, 0, unroll=16)
     early()
-    lax.fori_loop(groups // 2, groups, group, 0, unroll=4)
+    lax.fori_loop(groups // 2, groups, group, 0, unroll=16)
     fetch_tables()
     lane = quotient(lax.broadcasted_iota(jnp.int32, (groups, SIDE), 1), FINE)
     strips = [
@@ -349,19 +349,16 @@
     own.wait()
     for j in range(1, sub_count):
         expect_half(j).wait_recv()
-    step = 256
-
-    @pl.loop(0, degrees // step)
-    def _(n):
-        columns = pl.ds(pl.multiple_of(n * step, step), step)
+    step = 512
+    for first in range(0, degrees, step):
+        columns = slice(first, first + step)
         result = None
         for h in range(sub_count):
-            term = dot(left[h], halves[h, :, columns])
+            term = jnp.dot(left[h], halves[h, :, columns], preferred_element_type=jnp.float32)
             result = term if result is None else result + term
         result = result[: per * span] + result[per * span :]
         for i in range(per):
             out_ref[i, :, :, columns] = result[i * span : (i + 1) * span].reshape(orders, 2, step)
-
     for j in range(1, sub_count):
         half(j).wait_send()
 

time: 16.5 us -> 14.8 us (0.90)
  Pallas kernels: 15.4 us -> 13.7 us
    pallas_call x1, Pallas kernels: 15.4 us -> 13.7 us  [body(): pl.pallas_call(functools.partial(kernel, (shell_count, sky_count, sub_cou...]
where the time goes in v6:
time: 14.8 us; the launch traced here: 14.7 us
  Pallas kernels  13.7 us (93%)
  local copies, waits for them, and re-layouts  0.97 us (7%)
    pallas_call x1, Pallas kernels, body(): pl.pallas_call(functools.partial(kernel, (shell_count, sky_count, sub_cou...  13.7 us
    unnamed x1, local copies, waits for them, and re-layouts  0.97 us

profile of v6, /device:TPU:0, one launch (start us, length us, event | category | flops | bytes accessed | tf_op | source)
XLA Modules:
  0.0 14.7 jit_solution(10670567875960662976)
XLA Ops:
  0.0 13.7 %modes.1 = f32[2,32,2,2048]{3,2,1,0:T(2,128)S(1)} custom-call(s32[256,256]{1,0:T(8,128)} %bitcast.6, s32[256,256]{1,0:T(8,128)} %bitcast.7, f32[256,256]{1,0:T(8,128)} %bitcast.8, s32[1,256]{1,0:T(1,128)} %bitcast.9, s32[1,256]{1,0:T(1,128)} %shell_hbm.1, s32[1,256]{1,0:T(1,128)} %place_hbm.1, f32[256,256]{1,0:T(8,128)} %constant.4.clone.spectrum_hbm, ...), custom_call_target="tpu_custom_call" | custom-call | tf_op jit(solution)/shard_map/modes/pallas_call | solution.py:394
  13.7 1.0 %copy.12 = f32[2,32,2,2048]{3,2,1,0:T(2,128)} copy(f32[2,32,2,2048]{3,2,1,0:T(2,128)S(1)} %modes.1) | data formatting | bytes 2097152

commit v7 on v6

--- a/solution.py
+++ b/solution.py
@@ -114,9 +114,8 @@
             hist_ref[side, at, :] = own[:, side * SIDE : (side + 1) * SIDE]
         return carry
 
-    lax.fori_loop(0, groups // 2, group, 0, unroll=16)
+    lax.fori_loop(0, groups, group, 0, unroll=32)
     early()
-    lax.fori_loop(groups // 2, groups, group, 0, unroll=16)
     fetch_tables()
     lane = quotient(lax.broadcasted_iota(jnp.int32, (groups, SIDE), 1), FINE)
     strips = [
@@ -176,7 +175,8 @@
     spectrum_hbm, turns_hbm, weight_hbm, basis_ref, out_ref,
     cycle_ref, pixel_ref, mass_ref, block_ref, shell_ref, place_ref, spectrum_ref, turns_ref,
     weight_ref, key_ref, fine_ref, high_ref, low_ref, hist_ref, parts_ref,
-    halves, arrived, fetch_sem, own_sem, half_send, half_recv, part_send, part_recv,
+    halves, arrived, rounded, fetch_sem, own_sem, half_send, half_recv, part_send, part_recv,
+    sum_send, sum_recv,
 ):
     fetches = [
         pltpu.make_async_copy(source, target, fetch_sem.at[n])
@@ -207,6 +207,7 @@
     peers = shell_count * sky_count * sub_count
     me = (shell * sky_count + sky) * sub_count + sub
     degrees = halves.shape[2]
+    rows = arrived.shape[1]
     orders = basis_ref.shape[0] // cycles
 
     def place(rank):
@@ -227,7 +228,9 @@
     def send(j):
         target = place(rest(me + j, peers))
         return pltpu.make_async_remote_copy(
-            src_ref=parts_ref.at[target["sky"]],
+            src_ref=parts_ref.at[
+                target["sky"], pl.ds(pl.multiple_of(target["sub"] * rows, rows), rows)
+            ],
             dst_ref=arrived.at[me],
             send_sem=part_send.at[j],
             recv_sem=part_recv.at[j],
@@ -238,7 +241,7 @@
     def expect(j):
         source = rest(me + peers - j, peers)
         return pltpu.make_async_remote_copy(
-            src_ref=parts_ref.at[0],
+            src_ref=parts_ref.at[0, pl.ds(0, rows)],
             dst_ref=arrived.at[source],
             send_sem=part_send.at[j],
             recv_sem=part_recv.at[j],
@@ -298,17 +301,46 @@
     def _(j):
         send(j).start()
 
-    arrived[me] = parts_ref[sky]
+    arrived[me] = parts_ref[sky, pl.ds(pl.multiple_of(sub * rows, rows), rows)]
 
     @pl.loop(1, peers, unroll=peers <= 16)
     def _(j):
         expect(j).wait_recv()
 
     group = sky_count * sub_count
+    sums = [jnp.sum(arrived[x * group : (x + 1) * group], axis=0) for x in range(shell_count)]
+    modes = jnp.concatenate(sums, axis=0) * (2.0 * math.pi / NP)
+    rounded[sub] = modes.astype(jnp.bfloat16)
+
+    def hand(j):
+        return pltpu.make_async_remote_copy(
+            src_ref=rounded.at[sub],
+            dst_ref=rounded.at[sub],
+            send_sem=sum_send.at[j],
+            recv_sem=sum_recv.at[j],
+            device_id={"sub": rest(sub + j, sub_count)},
+            device_id_type=MESH,
+        )
+
+    def expect_sum(j):
+        source = rest(sub + sub_count - j, sub_count)
+        return pltpu.make_async_remote_copy(
+            src_ref=rounded.at[sub],
+            dst_ref=rounded.at[source],
+            send_sem=sum_send.at[j],
+            recv_sem=sum_recv.at[j],
+            device_id={"sub": source},
+            device_id_type=MESH,
+        )
+
+    for j in range(1, sub_count):
+        hand(j).start()
+    for j in range(1, sub_count):
+        expect_sum(j).wait_recv()
+    summed = [rounded[c].astype(jnp.float32) for c in range(sub_count)]
     folded = [None] * per
     for x in range(shell_count):
-        total = jnp.sum(arrived[x * group : (x + 1) * group], axis=0)
-        modes = (total * (2.0 * math.pi / NP)).astype(jnp.bfloat16).astype(jnp.float32)
+        modes = jnp.concatenate([kept[x * rows : (x + 1) * rows] for kept in summed], axis=0)
         for s in range(SHELL_DEV):
             part = modes[s * blocks : (s + 1) * blocks]
             lens = x * SHELL_DEV + s
@@ -337,15 +369,15 @@
     turn = quotient(rest(lane, cycles), CYCLE_DEV)
     left = []
     for h in range(sub_count):
-        rows = []
+        strips = []
         for piece in range(2):
             for i in range(per):
                 block = (piece * per + i) * blocks + h * (cycles // CYCLE_DEV) + turn
                 pick = jnp.where(row == block, 1.0, 0.0).astype(jnp.bfloat16)
                 spread = dot(coefficients, pick)
                 chosen = jnp.where(even, spread[:span], spread[span:])
-                rows.append(jnp.where(diagonal, chosen, 0.0).astype(jnp.bfloat16))
-        left.append(jnp.concatenate(rows, axis=0))
+                strips.append(jnp.where(diagonal, chosen, 0.0).astype(jnp.bfloat16))
+        left.append(jnp.concatenate(strips, axis=0))
     own.wait()
     for j in range(1, sub_count):
         expect_half(j).wait_recv()
@@ -361,6 +393,7 @@
             out_ref[i, :, :, columns] = result[i * span : (i + 1) * span].reshape(orders, 2, step)
     for j in range(1, sub_count):
         half(j).wait_send()
+        hand(j).wait_send()
 
     @pl.loop(1, peers, unroll=peers <= 16)
     def _(j):
@@ -413,13 +446,16 @@
             pltpu.VMEM((2, tiles * CYCLE_DEV * TP // (2 * SIDE), SIDE), jnp.float32),
             pltpu.VMEM((sky_count, bins, width), jnp.float32),
             pltpu.VMEM((sub_count, orders * cycles, share), jnp.bfloat16),
-            pltpu.VMEM((peers, bins, width), jnp.float32),
+            pltpu.VMEM((peers, bins // sub_count, width), jnp.float32),
+            pltpu.VMEM((sub_count, shell_count * bins // sub_count, width), jnp.bfloat16),
             pltpu.SemaphoreType.DMA((3 * (particles // SIDE) + 6,)),
             pltpu.SemaphoreType.DMA,
             pltpu.SemaphoreType.DMA((sub_count,)),
             pltpu.SemaphoreType.DMA((sub_count,)),
             pltpu.SemaphoreType.DMA((peers,)),
             pltpu.SemaphoreType.DMA((peers,)),
+            pltpu.SemaphoreType.DMA((sub_count,)),
+            pltpu.SemaphoreType.DMA((sub_count,)),
         ],
         compiler_params=pltpu.CompilerParams(
             collective_id=0, has_side_effects=True, vmem_limit_bytes=60 << 20

time: 14.8 us -> 15 us (1.014)
  Pallas kernels: 13.7 us -> 13.9 us
    pallas_call x1, Pallas kernels: 13.7 us -> 13.9 us  [body(): pl.pallas_call(functools.partial(kernel, (shell_count, sky_count, sub_cou...]
where the time goes in v7:
time: 15 us; the launch traced here: 14.8 us
  Pallas kernels  13.9 us (93%)
  local copies, waits for them, and re-layouts  0.97 us (6%)
    pallas_call x1, Pallas kernels, body(): pl.pallas_call(functools.partial(kernel, (shell_count, sky_count, sub_cou...  13.9 us
    unnamed x1, local copies, waits for them, and re-layouts  0.97 us

profile of v7, /device:TPU:0, one launch (start us, length us, event | category | flops | bytes accessed | tf_op | source)
XLA Modules:
  0.0 14.8 jit_solution(7741761972996855359)
XLA Ops:
  0.0 13.9 %modes.1 = f32[2,32,2,2048]{3,2,1,0:T(2,128)S(1)} custom-call(s32[256,256]{1,0:T(8,128)} %bitcast.6, s32[256,256]{1,0:T(8,128)} %bitcast.7, f32[256,256]{1,0:T(8,128)} %bitcast.8, s32[1,256]{1,0:T(1,128)} %bitcast.9, s32[1,256]{1,0:T(1,128)} %shell_hbm.1, s32[1,256]{1,0:T(1,128)} %place_hbm.1, f32[256,256]{1,0:T(8,128)} %constant.4.clone.spectrum_hbm, ...), custom_call_target="tpu_custom_call" | custom-call | tf_op jit(solution)/shard_map/modes/pallas_call | solution.py:427
  13.9 1.0 %copy.12 = f32[2,32,2,2048]{3,2,1,0:T(2,128)} copy(f32[2,32,2,2048]{3,2,1,0:T(2,128)S(1)} %modes.1) | data formatting | bytes 2097152

commit v8 on v6

--- a/solution.py
+++ b/solution.py
@@ -114,9 +114,8 @@
             hist_ref[side, at, :] = own[:, side * SIDE : (side + 1) * SIDE]
         return carry
 
-    lax.fori_loop(0, groups // 2, group, 0, unroll=16)
+    lax.fori_loop(0, groups, group, 0, unroll=32)
     early()
-    lax.fori_loop(groups // 2, groups, group, 0, unroll=16)
     fetch_tables()
     lane = quotient(lax.broadcasted_iota(jnp.int32, (groups, SIDE), 1), FINE)
     strips = [
@@ -298,6 +297,27 @@
     def _(j):
         send(j).start()
 
+    width = parts_ref.shape[2]
+    to = lax.broadcasted_iota(jnp.int32, (width, width), 0)
+    within = rest(to, 2 * orders)
+    source = to - within + rest(to, 2) * orders + quotient(within, 2)
+    swap = source == lax.broadcasted_iota(jnp.int32, (width, width), 1)
+    swap = jnp.where(swap, 1.0, 0.0).astype(jnp.bfloat16)
+    depth = orders * cycles
+    span = 2 * orders
+    lane = lax.broadcasted_iota(jnp.int32, (2 * per * blocks, depth), 1)
+    row = lax.broadcasted_iota(jnp.int32, (2 * per * blocks, depth), 0)
+    lane_out = lax.broadcasted_iota(jnp.int32, (span, depth), 1)
+    diagonal = quotient(lane_out, cycles) == quotient(
+        lax.broadcasted_iota(jnp.int32, (span, depth), 0), 2
+    )
+    even = rest(lane_out, CYCLE_DEV) == 0
+    turn = quotient(rest(lane, cycles), CYCLE_DEV)
+    picks = []
+    for h in range(sub_count):
+        for place_of in range(2 * per):
+            block = place_of * blocks + h * (cycles // CYCLE_DEV) + turn
+            picks.append(jnp.where(row == block, 1.0, 0.0).astype(jnp.bfloat16))
     arrived[me] = parts_ref[sky]
 
     @pl.loop(1, peers, unroll=peers <= 16)
@@ -318,31 +338,13 @@
                 term = weight * part
                 folded[i] = term if folded[i] is None else folded[i] + term
     folded = jnp.concatenate(split(jnp.concatenate(folded, axis=0)), axis=0)
-    width = folded.shape[1]
-    to = lax.broadcasted_iota(jnp.int32, (width, width), 0)
-    within = rest(to, 2 * orders)
-    source = to - within + rest(to, 2) * orders + quotient(within, 2)
-    swap = source == lax.broadcasted_iota(jnp.int32, (width, width), 1)
-    swap = jnp.where(swap, 1.0, 0.0).astype(jnp.bfloat16)
     coefficients = dot(swap, folded, 1).astype(jnp.bfloat16)
-    depth = orders * cycles
-    span = 2 * orders
-    lane = lax.broadcasted_iota(jnp.int32, (2 * per * blocks, depth), 1)
-    row = lax.broadcasted_iota(jnp.int32, (2 * per * blocks, depth), 0)
-    lane_out = lax.broadcasted_iota(jnp.int32, (span, depth), 1)
-    diagonal = quotient(lane_out, cycles) == quotient(
-        lax.broadcasted_iota(jnp.int32, (span, depth), 0), 2
-    )
-    even = rest(lane_out, CYCLE_DEV) == 0
-    turn = quotient(rest(lane, cycles), CYCLE_DEV)
     left = []
     for h in range(sub_count):
         rows = []
         for piece in range(2):
             for i in range(per):
-                block = (piece * per + i) * blocks + h * (cycles // CYCLE_DEV) + turn
-                pick = jnp.where(row == block, 1.0, 0.0).astype(jnp.bfloat16)
-                spread = dot(coefficients, pick)
+                spread = dot(coefficients, picks[(h * 2 + piece) * per + i])
                 chosen = jnp.where(even, spread[:span], spread[span:])
                 rows.append(jnp.where(diagonal, chosen, 0.0).astype(jnp.bfloat16))
         left.append(jnp.concatenate(rows, axis=0))

time: 14.8 us -> 14.3 us (0.966)
  Pallas kernels: 13.7 us -> 13.2 us
    pallas_call x1, Pallas kernels: 13.7 us -> 13.2 us  [body(): pl.pallas_call(functools.partial(kernel, (shell_count, sky_count, sub_cou...]
where the time goes in v8:
time: 14.3 us; the launch traced here: 14.1 us
  Pallas kernels  13.2 us (92%)
  local copies, waits for them, and re-layouts  0.97 us (7%)
    pallas_call x1, Pallas kernels, body(): pl.pallas_call(functools.partial(kernel, (shell_count, sky_count, sub_cou...  13.2 us
    unnamed x1, local copies, waits for them, and re-layouts  0.97 us

profile of v8, /device:TPU:0, one launch (start us, length us, event | category | flops | bytes accessed | tf_op | source)
XLA Modules:
  0.0 14.1 jit_solution(2752904998989001195)
XLA Ops:
  0.0 13.2 %modes.1 = f32[2,32,2,2048]{3,2,1,0:T(2,128)S(1)} custom-call(s32[256,256]{1,0:T(8,128)} %bitcast.6, s32[256,256]{1,0:T(8,128)} %bitcast.7, f32[256,256]{1,0:T(8,128)} %bitcast.8, s32[1,256]{1,0:T(1,128)} %bitcast.9, s32[1,256]{1,0:T(1,128)} %shell_hbm.1, s32[1,256]{1,0:T(1,128)} %place_hbm.1, f32[256,256]{1,0:T(8,128)} %constant.4.clone.spectrum_hbm, ...), custom_call_target="tpu_custom_call" | custom-call | tf_op jit(solution)/shard_map/modes/pallas_call | solution.py:396
  13.2 1.0 %copy.12 = f32[2,32,2,2048]{3,2,1,0:T(2,128)} copy(f32[2,32,2,2048]{3,2,1,0:T(2,128)S(1)} %modes.1) | data formatting | bytes 2097152
